TPU v7x, 128 devices: a whole 4x4x4 slice. The times are simulated.
128 devices in a mesh: expert: 8 (over z_lo, y), dp: 16 (over z_hi, x, core).
Axes of the slice: x: 4, y: 4, z: 4 (z_hi: 2, z_lo: 2; z = z_hi * 2 + z_lo), core: 2. Of those that a mesh axis runs over, the one named last changes fastest.
Arguments:
- tokens: bfloat16 [2048, 7168], P('dp', 'expert'), may hold values from -6 to 6
- grad_out: bfloat16 [2048, 7168], P('dp', 'expert'), may hold values from -6 to 6
- expert_ids: int32 [2048, 2], P('dp'), may hold values from -1 to 7, as said below
- route_weights: float32 [2048, 2], P('dp'), may hold values from 0.1 to 1
- w_gate: bfloat16 [8, 7168, 2048], P('expert', 'dp'), may hold values from -0.0625 to 0.0625
- w_up: bfloat16 [8, 7168, 2048], P('expert', 'dp'), may hold values from -0.0625 to 0.0625
- w_down: bfloat16 [8, 2048, 7168], P('expert', None, 'dp'), may hold values from -0.125 to 0.125
Outputs:
- grad_tokens: bfloat16 [2048, 7168], P('dp', 'expert')
- grad_gate: bfloat16 [8, 7168, 2048], P('expert', 'dp')
- grad_up: bfloat16 [8, 7168, 2048], P('expert', 'dp')
- grad_down: bfloat16 [8, 2048, 7168], P('expert', None, 'dp')
Inputs may be any that keep to these rules, and one draw needn't show every extreme that they name: expert_ids[t, 0] is an expert; expert_ids[t, 1] is another expert or -1. Within each block of 128 rows (the tokens of one index of dp) no expert appears in more than 64 rows, and one expert, the same in every block, appears in exactly 64 rows, each of which has -1 as its second entry.
All inputs are finite; a program needn't handle non-finite values.
Results may differ from a plain program's by a relative error of at most 0.03.
Values may be sent and summed in bfloat16 or wider, within the bound.
A program may use at most 128 MiB of HBM per device.

v0:
```python
import math

import jax
import jax.numpy as jnp
from jax import lax
from jax.sharding import PartitionSpec as P


def body(tokens, grad_out, expert_ids, route_weights, w_gate, w_up, w_down):
    experts = lax.axis_size("expert")
    groups = lax.axis_size("dp")
    tok_rows = tokens.shape[0]
    capacity = tok_rows // 2
    hidden = w_gate.shape[2]
    slots = groups * capacity
    expert_index = lax.axis_index("expert")
    inv_root = 1.0 / math.sqrt(tok_rows * groups)
    rows_first = (((0,), (0,)), ((), ()))
    last_dims = (((1,), (1,)), ((), ()))
    routed = expert_ids >= 0
    matches = (
        expert_ids[:, :, None] == jnp.arange(experts, dtype=jnp.int32)[None, None, :]
    ).astype(jnp.int32)
    flat_match = matches.reshape(tok_rows * 2, experts)
    position = jnp.sum(flat_match * (jnp.cumsum(flat_match, axis=0) - 1), axis=1).reshape(
        tok_rows, 2
    )
    slot_ids = jnp.where(routed, expert_ids * capacity + position, -1)
    slot_match = (
        slot_ids[None, :, :] == jnp.arange(experts * capacity, dtype=jnp.int32)[:, None, None]
    ).astype(jnp.float32)
    dispatch = jnp.sum(slot_match, axis=2).astype(jnp.bfloat16)
    slot_weight = jnp.einsum("stk,tk->s", slot_match, route_weights)
    own_weight = lax.dynamic_slice_in_dim(slot_weight, expert_index * capacity, capacity)
    send_x = (
        jnp.dot(dispatch, tokens, preferred_element_type=jnp.float32)
        .astype(jnp.bfloat16)
        .reshape(experts, capacity, -1)
    )
    send_g = (
        jnp.dot(dispatch, grad_out, preferred_element_type=jnp.float32)
        .astype(jnp.bfloat16)
        .reshape(experts, capacity, -1)
    )
    recv_x, recv_g = (
        lax.all_to_all(
            lax.all_to_all(send_x, "expert", split_axis=0, concat_axis=2, tiled=True),
            "dp",
            split_axis=2,
            concat_axis=1,
            tiled=True,
        ),
        lax.all_to_all(
            lax.all_to_all(send_g, "expert", split_axis=0, concat_axis=2, tiled=True),
            "dp",
            split_axis=2,
            concat_axis=1,
            tiled=True,
        ),
    )
    feature_rows = recv_x.reshape(slots, -1)
    grad_rows = recv_g.reshape(slots, -1)
    gate_shard = w_gate[0]
    up_shard = w_up[0]
    down_shard = w_down[0]
    shard_width = gate_shard.shape[0]
    x_block = feature_rows
    g_block = grad_rows
    gate = jnp.dot(x_block, gate_shard, preferred_element_type=jnp.float32)
    upper = jnp.dot(x_block, up_shard, preferred_element_type=jnp.float32)
    back = lax.dot_general(g_block, down_shard, last_dims, preferred_element_type=jnp.float32)
    mine = lax.psum_scatter(
        jnp.concatenate([gate, upper, back], axis=1).astype(jnp.bfloat16),
        "dp",
        scatter_dimension=0,
        tiled=True,
    ).astype(jnp.float32)
    gate = mine[:, :hidden]
    upper = mine[:, hidden : 2 * hidden]
    back = mine[:, 2 * hidden :] * own_weight[:, None]
    sigmoid_gate = jax.nn.sigmoid(gate)
    scaled = own_weight[:, None] * gate * sigmoid_gate * upper
    d_gate = back * upper * sigmoid_gate * (1.0 + gate * (1.0 - sigmoid_gate))
    d_up = back * gate * sigmoid_gate
    local = jnp.concatenate([scaled, d_gate, d_up], axis=1).astype(jnp.bfloat16)
    piece = lax.all_gather(local, "dp", axis=0, tiled=True)
    x_block = feature_rows
    g_block = grad_rows
    scaled = piece[:, :hidden]
    d_gate = piece[:, hidden : 2 * hidden]
    d_up = piece[:, 2 * hidden :]
    grad_g = lax.dot_general(x_block, d_gate, rows_first, preferred_element_type=jnp.float32)
    grad_u = lax.dot_general(x_block, d_up, rows_first, preferred_element_type=jnp.float32)
    grad_d = lax.dot_general(scaled, g_block, rows_first, preferred_element_type=jnp.float32)
    block_dx = lax.dot_general(
        d_gate, gate_shard, last_dims, preferred_element_type=jnp.float32
    ) + lax.dot_general(d_up, up_shard, last_dims, preferred_element_type=jnp.float32)
    dx_rows = block_dx.astype(jnp.bfloat16)
    grad_g, grad_u, grad_d, dx_rows = (grad_g, grad_u, grad_d, dx_rows)
    returned = lax.all_to_all(
        lax.all_to_all(
            dx_rows.reshape(1, slots, shard_width), "dp", split_axis=1, concat_axis=2, tiled=True
        ),
        "expert",
        split_axis=2,
        concat_axis=0,
        tiled=True,
    )
    returned = returned.reshape(experts * capacity, -1)
    grad_tokens = lax.dot_general(
        dispatch, returned, rows_first, preferred_element_type=jnp.float32
    ).astype(jnp.bfloat16)
    grad_gate = (grad_g * inv_root).astype(jnp.bfloat16)[None]
    grad_up = (grad_u * inv_root).astype(jnp.bfloat16)[None]
    grad_down = (grad_d * inv_root).astype(jnp.bfloat16)[None]
    return (grad_tokens, grad_gate, grad_up, grad_down)


def solution(mesh):
    in_specs = (
        P("dp", "expert"),
        P("dp", "expert"),
        P("dp", None),
        P("dp", None),
        P("expert", "dp", None),
        P("expert", "dp", None),
        P("expert", None, "dp"),
    )
    out_specs = (
        P("dp", "expert"),
        P("expert", "dp", None),
        P("expert", "dp", None),
        P("expert", None, "dp"),
    )
    return jax.shard_map(body, mesh=mesh, in_specs=in_specs, out_specs=out_specs, check_vma=False)
```

profile of v0, /device:TPU:1, one launch (start us, length us, event | category | flops | bytes accessed | tf_op | source)
XLA Modules:
  0.0 595.4 jit_solution(15682744833489243268)
XLA Ops:
  12.6 6.4 %all-to-all-start.2 = ((bf16[8,64,896]{2,1,0:T(8,128)(2,1)}), bf16[8,64,896]{2,1,0:T(8,128)(2,1)S(1)}, u32[]{:S(2)}, u32[]{:S(2)}) async-start(bf16[8,64,896]{2,1,0:T(8,128)(2,1)} %bitcast.12), calls=%async_computation.2 | async-start | bytes 1835008 | tf_op jit(solution)/shard_map/all_to_all | solution.py:54
  20.3 13.1 %all-to-all-done.2 = bf16[8,64,896]{2,1,0:T(8,128)(2,1)S(1)} async-done(((bf16[8,64,896]{2,1,0:T(8,128)(2,1)}), bf16[8,64,896]{2,1,0:T(8,128)(2,1)S(1)}, u32[]{:S(2)}, u32[]{:S(2)}) %all-to-all-start.2) | async-done | bytes 917536 | tf_op jit(solution)/shard_map/all_to_all | solution.py:54
  40.4 11.1 %reshape.65 = bf16[1,64,7168]{1,0,2:T(2,128)(2,1)} reshape(bf16[1,64,8,896]{1,3,2,0:T(8,128)(2,1)} %copy.97) | data formatting | bytes 1835008 | tf_op jit(solution)/shard_map/all_to_all | solution.py:54
  52.1 41.0 %reduce.2 = bf16[7168,64]{1,0:T(8,128)(2,1)} reduce(bf16[7168,1,64]{2,1,0:T(2,128)(2,1)} %bitcast.92, bf16[]{:T(256)} %broadcast.46), dimensions={1}, to_apply=%bitcast.70.reduce_sub_computation | reduce | bytes 1835010
  97.3 8.5 %all-to-all-start.3 = ((bf16[16,2,14336]{2,1,0:T(2,128)(2,1)}), bf16[16,2,14336]{2,1,0:T(2,128)(2,1)}, u32[]{:S(2)}, u32[]{:S(2)}) async-start(bf16[16,2,14336]{2,1,0:T(2,128)(2,1)} %reshape.68), calls=%async_computation.3 | async-start | bytes 1835008 | tf_op jit(solution)/shard_map/all_to_all | solution.py:53
  107.5 11.1 %reshape.64 = bf16[1,64,7168]{1,0,2:T(2,128)(2,1)} reshape(bf16[1,64,8,896]{1,3,2,0:T(8,128)(2,1)} %copy.96) | data formatting | bytes 1835008 | tf_op jit(solution)/shard_map/all_to_all | solution.py:47
  118.7 41.0 %reduce.3 = bf16[7168,64]{1,0:T(8,128)(2,1)} reduce(bf16[7168,1,64]{2,1,0:T(2,128)(2,1)} %bitcast.94, bf16[]{:T(256)} %broadcast.46), dimensions={1}, to_apply=%bitcast.72.reduce_sub_computation | reduce | bytes 1835010
  163.9 7.2 %all-to-all-start.1 = ((bf16[16,2,14336]{2,1,0:T(2,128)(2,1)}), bf16[16,2,14336]{2,1,0:T(2,128)(2,1)}, u32[]{:S(2)}, u32[]{:S(2)}) async-start(bf16[16,2,14336]{2,1,0:T(2,128)(2,1)} %reshape.70), calls=%async_computation.1 | async-start | bytes 1835008 | tf_op jit(solution)/shard_map/all_to_all | solution.py:46
  171.6 9.9 %reshape.69 = bf16[7168,1,64]{2,1,0:T(2,128)(2,1)} reshape(bf16[16,2,14336]{2,1,0:T(2,128)(2,1)} %all-to-all-done.3) | data formatting | bytes 1835008
  181.5 8.1 %copy.88 = bf16[1,64,7168]{2,1,0:T(8,128)(2,1)} copy(bf16[1,64,7168]{1,0,2:T(2,128)(2,1)} %bitcast.95) | data formatting | bytes 1835008 | tf_op jit(solution)/shard_map/all_to_all | solution.py:53
  193.6 9.9 %reshape.71 = bf16[7168,1,64]{2,1,0:T(2,128)(2,1)} reshape(bf16[16,2,14336]{2,1,0:T(2,128)(2,1)} %all-to-all-done.1) | data formatting | bytes 1835008
  203.5 8.1 %copy.84 = bf16[1,64,7168]{2,1,0:T(8,128)(2,1)} copy(bf16[1,64,7168]{1,0,2:T(2,128)(2,1)} %bitcast.96) | data formatting | bytes 1835008 | tf_op jit(solution)/shard_map/all_to_all | solution.py:46
  221.7 11.3 %pad_maximum_fusion = bf16[1024,6144]{1,0:T(8,128)(2,1)} fusion(bf16[1024,2048]{1,0:T(8,128)(2,1)S(1)} %convolution_convert_fusion, bf16[1024,2048]{1,0:T(8,128)(2,1)S(1)} %convolution_convert_fusion.1, bf16[1024,2048]{1,0:T(8,128)(2,1)S(1)} %convolution_convert_fusion.2), kind=kLoop, calls=%fused_computation | loop fusion | flops 37748736 | bytes 25165824 | tf_op jit(solution)/shard_map/concatenate | solution.py:73
  234.0 122.2 %reduce-scatter.2.cloned.1.call-done = bf16[64,6144]{1,0:T(8,128)(2,1)} async-done(((bf16[1024,6144]{1,0:T(8,128)(2,1)}), bf16[64,6144]{1,0:T(8,128)(2,1)}) %reduce-scatter.2.cloned.1.call-update) | async-done | bytes 786448 | tf_op jit(solution)/shard_map/reduce_scatter | solution.py:72
  358.8 91.2 %all-gather.2.cloned.1.call-done = bf16[1024,6144]{1,0:T(8,128)(2,1)} async-done(((bf16[64,6144]{1,0:T(8,128)(2,1)}), bf16[1024,6144]{1,0:T(8,128)(2,1)}) %all-gather.2.cloned.1.call-update) | async-done | bytes 12582928 | tf_op jit(solution)/shard_map/all_gather | solution.py:86
  449.9 4.4 fusion.4
  462.6 8.3 %reduce.4 = bf16[1024,448]{1,0:T(8,128)(2,1)S(1)} reduce(bf16[1024,1,448]{2,1,0:T(2,128)(2,1)} %bitcast.98, bf16[]{:T(256)} %broadcast.46), dimensions={1}, to_apply=%bitcast.74.reduce_sub_computation | reduce | bytes 1835010
  476.9 5.8 fusion.16
  482.7 10.2 %all-to-all-done.4 = bf16[16,2,14336]{2,1,0:T(2,128)(2,1)S(1)} async-done(((bf16[16,2,14336]{2,1,0:T(2,128)(2,1)}), bf16[16,2,14336]{2,1,0:T(2,128)(2,1)S(1)}, u32[]{:S(2)}, u32[]{:S(2)}) %all-to-all-start.4) | async-done | bytes 917536 | tf_op jit(solution)/shard_map/all_to_all | solution.py:101
  500.2 11.1 %reshape.66 = bf16[1,64,7168]{1,0,2:T(2,128)(2,1)} reshape(bf16[1,64,16,448]{1,3,2,0:T(8,128)(2,1)} %copy.98) | data formatting | bytes 1835008 | tf_op jit(solution)/shard_map/all_to_all | solution.py:101
  511.3 41.0 %reduce.5 = bf16[7168,64]{1,0:T(8,128)(2,1)} reduce(bf16[7168,1,64]{2,1,0:T(2,128)(2,1)} %bitcast.93, bf16[]{:T(256)} %broadcast.46), dimensions={1}, to_apply=%bitcast.76.reduce_sub_computation | reduce | bytes 1835010
  561.0 5.9 fusion.19
  566.9 5.5 fusion.22
  579.5 7.2 %copy.93 = bf16[1,64,7168]{2,1,0:T(8,128)(2,1)S(1)} copy(bf16[1,64,7168]{1,0,2:T(2,128)(2,1)} %bitcast.97) | data formatting | bytes 1835008 | tf_op jit(solution)/shard_map/all_to_all | solution.py:100
  (75 shorter events, 80.9 us)
Async XLA Ops:
  7.2 207.4 %copy-start = (bf16[1,448,2048]{2,1,0:T(8,128)(2,1)S(1)}, bf16[1,448,2048]{2,1,0:T(8,128)(2,1)}, u32[]{:S(2)}) copy-start(bf16[1,448,2048]{2,1,0:T(8,128)(2,1)} %param.12) | copy-start | bytes 5505028
  7.2 11.8 %copy-start.5 = (bf16[128,896]{1,0:T(8,128)(2,1)S(1)}, bf16[128,896]{1,0:T(8,128)(2,1)}, u32[]{:S(2)}) copy-start(bf16[128,896]{1,0:T(8,128)(2,1)} %param.7) | copy-start | bytes 688132
  12.6 20.8 %all-to-all-start.2 = ((bf16[8,64,896]{2,1,0:T(8,128)(2,1)}), bf16[8,64,896]{2,1,0:T(8,128)(2,1)S(1)}, u32[]{:S(2)}, u32[]{:S(2)}) async-start(bf16[8,64,896]{2,1,0:T(8,128)(2,1)} %bitcast.12), calls=%async_computation.2 | async-start | bytes 1835008 | tf_op jit(solution)/shard_map/all_to_all | solution.py:54
  33.4 0.9 copy-start.1
  34.3 63.0 %all-to-all-start = ((bf16[8,64,896]{2,1,0:T(8,128)(2,1)}), bf16[8,64,896]{2,1,0:T(8,128)(2,1)S(1)}, u32[]{:S(2)}, u32[]{:S(2)}) async-start(bf16[8,64,896]{2,1,0:T(8,128)(2,1)} %bitcast.5), calls=%async_computation | async-start | bytes 1835008 | tf_op jit(solution)/shard_map/all_to_all | solution.py:47
  97.3 66.6 %all-to-all-start.3 = ((bf16[16,2,14336]{2,1,0:T(2,128)(2,1)}), bf16[16,2,14336]{2,1,0:T(2,128)(2,1)}, u32[]{:S(2)}, u32[]{:S(2)}) async-start(bf16[16,2,14336]{2,1,0:T(2,128)(2,1)} %reshape.68), calls=%async_computation.3 | async-start | bytes 1835008 | tf_op jit(solution)/shard_map/all_to_all | solution.py:53
  163.9 29.7 %all-to-all-start.1 = ((bf16[16,2,14336]{2,1,0:T(2,128)(2,1)}), bf16[16,2,14336]{2,1,0:T(2,128)(2,1)}, u32[]{:S(2)}, u32[]{:S(2)}) async-start(bf16[16,2,14336]{2,1,0:T(2,128)(2,1)} %reshape.70), calls=%async_computation.1 | async-start | bytes 1835008 | tf_op jit(solution)/shard_map/all_to_all | solution.py:46
  171.2 185.0 %reduce-scatter.2.cloned.1.call-start = ((), (), s32[]{:S(2)}) async-start(), calls=%async_computation.7 | async-start | bytes 13369344 | tf_op jit(solution)/shard_map/reduce_scatter | solution.py:72
  214.6 2.4 copy-start.4
  214.6 2.4 copy-start.7
  217.0 2.4 copy-start.2
  217.0 2.4 copy-start.6
  233.0 0.7 copy-start.9
  233.0 216.9 %all-gather.2.cloned.1.call-start = ((), (), s32[]{:S(2)}) async-start(), calls=%async_computation.8 | async-start | bytes 13369344 | tf_op jit(solution)/shard_map/all_gather | solution.py:86
  449.9 4.4 copy-start.8
  473.0 19.9 %all-to-all-start.4 = ((bf16[16,2,14336]{2,1,0:T(2,128)(2,1)}), bf16[16,2,14336]{2,1,0:T(2,128)(2,1)S(1)}, u32[]{:S(2)}, u32[]{:S(2)}) async-start(bf16[16,2,14336]{2,1,0:T(2,128)(2,1)} %reshape.72), calls=%async_computation.5 | async-start | bytes 1835008 | tf_op jit(solution)/shard_map/all_to_all | solution.py:101
  556.6 18.8 %all-to-all-start.5 = ((bf16[8,2,28672]{2,1,0:T(2,128)(2,1)}), bf16[8,2,28672]{2,1,0:T(2,128)(2,1)S(1)}, u32[]{:S(2)}, u32[]{:S(2)}) async-start(bf16[8,2,28672]{2,1,0:T(2,128)(2,1)} %reshape.74), calls=%async_computation.6 | async-start | bytes 1835008 | tf_op jit(solution)/shard_map/all_to_all | solution.py:100
  561.0 5.9 copy-start.3
Sparse Core Ops, SparseCore 0:
  233.1 123.0 reduce-scatter.1
  359.5 90.3 all-gather.1
where the time goes:
time: 606 us; the launch traced here: 595 us
  waiting for transfers between devices  240 us (40%)
  other arithmetic  147 us (24%)
  local copies, waits for them, and re-layouts  122 us (20%)
  matrix products  37.9 us (6%)
  starting transfers between devices  34.6 us (6%)
  between operations  14.8 us (2%)
    unnamed x4, other arithmetic  131 us
    reduce_scatter x1, waiting for transfers between devices, body(): lax.psum_scatter(jnp.concatenate([gate, upper, back], axis=1).astype(jnp....  122 us
    all_gather x1, waiting for transfers between devices, body(): piece = lax.all_gather(local, 'dp', axis=0, tiled=True)  91.2 us
    unnamed x32, local copies, waits for them, and re-layouts  47.4 us
    all_to_all x2, local copies, waits for them, and re-layouts, body(): lax.all_to_all(send_g, 'expert', split_axis=0, concat_axis=2, tiled=True)  13.7 us
    all_to_all x1, waiting for transfers between devices, body(): lax.all_to_all(send_g, 'expert', split_axis=0, concat_axis=2, tiled=True)  13.1 us
    all_to_all x2, local copies, waits for them, and re-layouts, body(): lax.all_to_all(dx_rows.reshape(1, slots, shard_width), 'dp', split_axis=1...  12.8 us
    all_to_all x2, local copies, waits for them, and re-layouts, body(): lax.all_to_all(send_x, 'expert', split_axis=0, concat_axis=2, tiled=True)  12.8 us
  transfers between devices with their start and end apart: 8, of which 5 were waited for; matrix products, arithmetic and copies ran while one was open for 26% of the time, Pallas kernels for 0%

commit v1 on v0

v1 whole, which is shorter than its diff:
```python
import math

import jax
import jax.numpy as jnp
from jax import lax
from jax.sharding import PartitionSpec as P


def body(tokens, grad_out, expert_ids, route_weights, w_gate, w_up, w_down):
    experts = lax.axis_size("expert")
    groups = lax.axis_size("dp")
    tok_rows, width = tokens.shape
    capacity = tok_rows // 2
    hidden = w_gate.shape[2]
    slots = groups * capacity
    expert_index = lax.axis_index("expert")
    inv_root = 1.0 / math.sqrt(tok_rows * groups)
    rows_first = (((0,), (0,)), ((), ()))
    last_dims = (((1,), (1,)), ((), ()))
    gate_shard, up_shard, down_shard = w_gate[0], w_up[0], w_down[0]
    shard = gate_shard.shape[0]
    halves = width // shard

    names = jnp.arange(experts, dtype=jnp.int32)[:, None]
    hit0 = expert_ids[:, 0][None, :] == names
    hit1 = expert_ids[:, 1][None, :] == names
    hit = (hit0 | hit1).astype(jnp.bfloat16)
    index = jnp.arange(tok_rows, dtype=jnp.int32)
    before = (index[:, None] < index[None, :]).astype(jnp.bfloat16)
    rank = jnp.dot(hit, before, preferred_element_type=jnp.float32)
    rank = jnp.where(hit > 0, rank, -1.0).astype(jnp.int32)
    chosen = rank[:, None, :] == jnp.arange(capacity, dtype=jnp.int32)[None, :, None]
    dispatch = chosen.astype(jnp.bfloat16).reshape(experts * capacity, tok_rows)
    weight_of = jnp.where(hit0, route_weights[:, 0][None, :], 0.0) + jnp.where(
        hit1, route_weights[:, 1][None, :], 0.0
    )
    own_rank = lax.dynamic_slice_in_dim(rank, expert_index, 1)
    own_weight_of = lax.dynamic_slice_in_dim(weight_of, expert_index, 1)
    own_weight = jnp.sum(
        jnp.where(
            own_rank == jnp.arange(capacity, dtype=jnp.int32)[:, None], own_weight_of, 0.0
        ),
        axis=1,
    )

    def send(rows):
        picked = [
            jnp.dot(
                dispatch,
                rows[:, h * shard : (h + 1) * shard],
                preferred_element_type=jnp.float32,
            )
            .astype(jnp.bfloat16)
            .reshape(experts, 1, capacity, shard)
            for h in range(halves)
        ]
        moved = lax.all_to_all(
            jnp.concatenate(picked, axis=1), "expert", split_axis=0, concat_axis=0, tiled=True
        )
        return lax.all_to_all(
            moved.reshape(groups, capacity, shard), "dp", split_axis=0, concat_axis=0, tiled=True
        ).reshape(slots, shard)

    x_block = send(tokens)
    g_block = send(grad_out)
    gate = jnp.dot(x_block, gate_shard, preferred_element_type=jnp.float32)
    upper = jnp.dot(x_block, up_shard, preferred_element_type=jnp.float32)
    back = lax.dot_general(g_block, down_shard, last_dims, preferred_element_type=jnp.float32)
    mine = lax.psum_scatter(
        jnp.concatenate([gate, upper, back], axis=1).astype(jnp.bfloat16),
        "dp",
        scatter_dimension=0,
        tiled=True,
    ).astype(jnp.float32)
    gate = mine[:, :hidden]
    upper = mine[:, hidden : 2 * hidden]
    back = mine[:, 2 * hidden :] * own_weight[:, None]
    sigmoid_gate = jax.nn.sigmoid(gate)
    scaled = own_weight[:, None] * gate * sigmoid_gate * upper
    d_gate = back * upper * sigmoid_gate * (1.0 + gate * (1.0 - sigmoid_gate))
    d_up = back * gate * sigmoid_gate
    local = jnp.concatenate([scaled, d_gate, d_up], axis=1).astype(jnp.bfloat16)
    piece = lax.all_gather(local, "dp", axis=0, tiled=True)
    scaled = piece[:, :hidden]
    d_gate = piece[:, hidden : 2 * hidden]
    d_up = piece[:, 2 * hidden :]
    block_dx = lax.dot_general(
        d_gate, gate_shard, last_dims, preferred_element_type=jnp.float32
    ) + lax.dot_general(d_up, up_shard, last_dims, preferred_element_type=jnp.float32)
    dx_rows = block_dx.astype(jnp.bfloat16)
    returned = lax.all_to_all(
        dx_rows.reshape(groups, capacity, shard), "dp", split_axis=0, concat_axis=0, tiled=True
    )
    returned = lax.all_to_all(
        returned.reshape(experts, halves, capacity, shard),
        "expert",
        split_axis=0,
        concat_axis=0,
        tiled=True,
    )
    grad_g = lax.dot_general(x_block, d_gate, rows_first, preferred_element_type=jnp.float32)
    grad_u = lax.dot_general(x_block, d_up, rows_first, preferred_element_type=jnp.float32)
    grad_d = lax.dot_general(scaled, g_block, rows_first, preferred_element_type=jnp.float32)
    grad_tokens = jnp.concatenate(
        [
            lax.dot_general(
                dispatch,
                returned[:, h].reshape(experts * capacity, shard),
                rows_first,
                preferred_element_type=jnp.float32,
            ).astype(jnp.bfloat16)
            for h in range(halves)
        ],
        axis=1,
    )
    grad_gate = (grad_g * inv_root).astype(jnp.bfloat16)[None]
    grad_up = (grad_u * inv_root).astype(jnp.bfloat16)[None]
    grad_down = (grad_d * inv_root).astype(jnp.bfloat16)[None]
    return (grad_tokens, grad_gate, grad_up, grad_down)


def solution(mesh):
    in_specs = (
        P("dp", "expert"),
        P("dp", "expert"),
        P("dp", None),
        P("dp", None),
        P("expert", "dp", None),
        P("expert", "dp", None),
        P("expert", None, "dp"),
    )
    out_specs = (
        P("dp", "expert"),
        P("expert", "dp", None),
        P("expert", "dp", None),
        P("expert", None, "dp"),
    )
    return jax.shard_map(body, mesh=mesh, in_specs=in_specs, out_specs=out_specs, check_vma=False)
```

time: 606 us -> 392 us (0.65); the launches traced: 595 us -> 391 us
  other arithmetic: 147 us -> 15.6 us
  local copies, waits for them, and re-layouts: 122 us -> 10.3 us
  blocking collectives: 0 us -> 45.1 us
  starting transfers between devices: 34.6 us -> 20.2 us
  matrix products: 37.9 us -> 47.8 us
    unnamed x4 -> x0, other arithmetic: 131 us -> none
    all_to_all x15 -> x0, local copies, waits for them, and re-layouts: 69.8 us -> none  [the longest x2 13.7 us: body(): lax.all_to_all(send_g, 'expert', split_axis=0, concat_axis=2, tiled=True)]
    unnamed x32 -> x17, local copies, waits for them, and re-layouts: 47.4 us -> 1.29 us
    all_to_all x0 -> x2, blocking collectives: none -> 45.1 us  [the longest x1 26 us: send(): lax.all_to_all(moved.reshape(groups, capacity, shard), 'dp', split_axis=0...]
    all_to_all x6 -> x4, starting transfers between devices: 34 us -> 20 us  [the longest x1 6.37 us: send(): lax.all_to_all(jnp.concatenate(picked, axis=1), 'expert', split_axis=0, c...]
    reduce_scatter x1, waiting for transfers between devices: 122 us -> 116 us  [body(): lax.psum_scatter(jnp.concatenate([gate, upper, back], axis=1).astype(jnp....]
    all_to_all x6 -> x4, waiting for transfers between devices: 26.2 us -> 30.8 us  [the longest x1 12 us: body(): lax.all_to_all(dx_rows.reshape(groups, capacity, shard), 'dp', split_axis...]
  transfers between devices with their start and end apart: 8 -> 6, of which waited for: 5 -> 6; matrix products, arithmetic and copies ran while one was open for 26% -> 9% of each run, Pallas kernels for 0% -> 0%
where the time goes in v1:
time: 392 us; the launch traced here: 391 us
  waiting for transfers between devices  238 us (61%)
  matrix products  47.8 us (12%)
  blocking collectives  45.1 us (12%)
  starting transfers between devices  20.2 us (5%)
  other arithmetic  15.6 us (4%)
  between operations  14.2 us (4%)
  local copies, waits for them, and re-layouts  10.3 us (3%)
    reduce_scatter x1, waiting for transfers between devices, body(): lax.psum_scatter(jnp.concatenate([gate, upper, back], axis=1).astype(jnp....  116 us
    all_gather x1, waiting for transfers between devices, body(): piece = lax.all_gather(local, 'dp', axis=0, tiled=True)  91.2 us
    all_to_all x1, blocking collectives, send(): lax.all_to_all(moved.reshape(groups, capacity, shard), 'dp', split_axis=0...  26 us
    all_to_all x1, blocking collectives, send(): lax.all_to_all(jnp.concatenate(picked, axis=1), 'expert', split_axis=0, c...  19.1 us
    all_to_all x1, waiting for transfers between devices, body(): lax.all_to_all(dx_rows.reshape(groups, capacity, shard), 'dp', split_axis...  12 us
    concatenate x1, other arithmetic, body(): jnp.concatenate([gate, upper, back], axis=1).astype(jnp.bfloat16)  11.4 us
  transfers between devices with their start and end apart: 6, of which 6 were waited for; matrix products, arithmetic and copies ran while one was open for 9% of the time, Pallas kernels for 0%

profile of v1, /device:TPU:1, one launch (start us, length us, event | category | flops | bytes accessed | tf_op | source)
XLA Modules:
  0.0 391.0 jit_solution(13324293775358559816)
XLA Ops:
  12.6 6.4 %all-to-all-start = ((bf16[8,2,64,448]{3,2,1,0:T(8,128)(2,1)}), bf16[8,2,64,448]{3,2,1,0:T(8,128)(2,1)S(1)}, u32[]{:S(2)}, u32[]{:S(2)}) async-start(bf16[8,2,64,448]{3,2,1,0:T(8,128)(2,1)} %copy.31), calls=%async_computation | async-start | bytes 2097152 | tf_op jit(solution)/shard_map/all_to_all | solution.py:57
  21.3 2.1 convolution_convert_fusion.3
  23.3 2.0 copy.33
  27.6 7.2 %all-to-all-done = bf16[8,2,64,448]{3,2,1,0:T(8,128)(2,1)S(1)} async-done(((bf16[8,2,64,448]{3,2,1,0:T(8,128)(2,1)}), bf16[8,2,64,448]{3,2,1,0:T(8,128)(2,1)S(1)}, u32[]{:S(2)}, u32[]{:S(2)}) %all-to-all-start) | async-done | bytes 917536 | tf_op jit(solution)/shard_map/all_to_all | solution.py:57
  34.7 19.1 %all_to_all.30 = bf16[8,2,64,448]{3,2,1,0:T(8,128)(2,1)} all-to-all(bf16[8,2,64,448]{3,2,1,0:T(8,128)(2,1)} %copy.34), channel_id=1, replica_groups=mesh['expert'=8,'dp'=16] {'expert'}, dimensions={0} | all-to-all | bytes 1835008 | tf_op jit(solution)/shard_map/all_to_all | solution.py:57
  53.8 26.0 %all_to_all.31 = bf16[16,64,448]{2,1,0:T(8,128)(2,1)} all-to-all(bf16[16,64,448]{2,1,0:T(8,128)(2,1)S(1)} %bitcast.62), channel_id=1, replica_groups=mesh['expert'=8,'dp'=16] {'dp'}, dimensions={0} | all-to-all | bytes 1835008 | tf_op jit(solution)/shard_map/all_to_all | solution.py:60
  79.9 5.2 %all-to-all-start.3 = ((bf16[16,64,448]{2,1,0:T(8,128)(2,1)}), bf16[16,64,448]{2,1,0:T(8,128)(2,1)}, u32[]{:S(2)}, u32[]{:S(2)}) async-start(bf16[16,64,448]{2,1,0:T(8,128)(2,1)} %bitcast.63), calls=%async_computation.3 | async-start | bytes 2097152 | tf_op jit(solution)/shard_map/all_to_all | solution.py:60
  85.1 5.7 %convolution_convert_fusion.1 = bf16[1024,2048]{1,0:T(8,128)(2,1)} fusion(bf16[1024,448]{1,0:T(8,128)(2,1)} %bitcast.70, bf16[1,448,2048]{2,1,0:T(8,128)(2,1)S(1)} %copy-done), kind=kOutput, calls=%fused_computation.4 | convolution fusion | flops 1881145344 | bytes 6946816 | tf_op jit(solution)/shard_map/dot_general | solution.py:67
  90.8 4.3 %convolution_convert_fusion.2 = bf16[1024,2048]{1,0:T(8,128)(2,1)} fusion(bf16[1024,448]{1,0:T(8,128)(2,1)S(1)} %bitcast.72, bf16[1,448,2048]{2,1,0:T(8,128)(2,1)S(1)} %copy-done.6), kind=kOutput, calls=%fused_computation.5 | convolution fusion | flops 1881145344 | bytes 6946816 | tf_op jit(solution)/shard_map/dot_general | solution.py:66
  95.1 7.5 %all-to-all-done.3 = bf16[16,64,448]{2,1,0:T(8,128)(2,1)} async-done(((bf16[16,64,448]{2,1,0:T(8,128)(2,1)}), bf16[16,64,448]{2,1,0:T(8,128)(2,1)}, u32[]{:S(2)}, u32[]{:S(2)}) %all-to-all-start.3) | async-done | bytes 917536 | tf_op jit(solution)/shard_map/all_to_all | solution.py:60
  102.6 4.3 %convolution_convert_fusion = bf16[1024,2048]{1,0:T(8,128)(2,1)S(1)} fusion(bf16[1024,448]{1,0:T(8,128)(2,1)} %bitcast.17, bf16[1,2048,448]{1,2,0:T(8,128)(2,1)} %param.13), kind=kOutput, calls=%fused_computation.3 | convolution fusion | flops 1881145344 | bytes 6946816 | tf_op jit(solution)/shard_map/dot_general | solution.py:68
  106.9 11.4 %pad_maximum_fusion = bf16[1024,6144]{1,0:T(8,128)(2,1)} fusion(bf16[1024,2048]{1,0:T(8,128)(2,1)S(1)} %convolution_convert_fusion, bf16[1024,2048]{1,0:T(8,128)(2,1)S(1)} %copy-done.1, bf16[1024,2048]{1,0:T(8,128)(2,1)S(1)} %copy-done.2), kind=kLoop, calls=%fused_computation | loop fusion | flops 37748736 | bytes 25165824 | tf_op jit(solution)/shard_map/concatenate | solution.py:70
  119.2 115.9 %reduce-scatter.2.cloned.1.call-done = bf16[64,6144]{1,0:T(8,128)(2,1)} async-done(((bf16[1024,6144]{1,0:T(8,128)(2,1)}), bf16[64,6144]{1,0:T(8,128)(2,1)}) %reduce-scatter.2.cloned.1.call-update) | async-done | bytes 786448 | tf_op jit(solution)/shard_map/reduce_scatter | solution.py:69
  237.6 91.2 %all-gather.2.cloned.1.call-done = bf16[1024,6144]{1,0:T(8,128)(2,1)} async-done(((bf16[64,6144]{1,0:T(8,128)(2,1)}), bf16[1024,6144]{1,0:T(8,128)(2,1)}) %all-gather.2.cloned.1.call-update) | async-done | bytes 12582928 | tf_op jit(solution)/shard_map/all_gather | solution.py:83
  328.8 4.4 %fusion.4 = f32[1024,448]{0,1:T(8,128)S(1)} fusion(bf16[1024,6144]{1,0:T(8,128)(2,1)} %all-gather.2.cloned.1.call-done, bf16[1,448,2048]{2,1,0:T(8,128)(2,1)S(1)} %copy-done), kind=kOutput, calls=%fused_computation.8 | convolution fusion | flops 1879048192 | bytes 7864320 | tf_op jit(solution)/shard_map/dot_general | solution.py:89
  333.2 5.3 %add_convert_fusion = bf16[1024,448]{0,1:T(8,128)(2,1)} fusion(f32[1024,448]{0,1:T(8,128)S(1)} %fusion.4, bf16[1,448,2048]{2,1,0:T(8,128)(2,1)S(1)} %copy-done.7, bf16[1024,6144]{1,0:T(8,128)(2,1)} %all-gather.2.cloned.1.call-done), kind=kOutput, calls=%fused_computation.25 | convolution fusion | flops 1879965696 | bytes 8781824 | tf_op jit(solution)/shard_map/dot_general | solution.py:87
  338.5 2.2 copy.35
  340.8 4.3 %all-to-all-start.4 = ((bf16[16,64,448]{2,1,0:T(8,128)(2,1)}), bf16[16,64,448]{2,1,0:T(8,128)(2,1)}, u32[]{:S(2)}, u32[]{:S(2)}) async-start(bf16[16,64,448]{2,1,0:T(8,128)(2,1)} %bitcast.19), calls=%async_computation.5 | async-start | bytes 2097152 | tf_op jit(solution)/shard_map/all_to_all | solution.py:91
  345.1 5.5 %fusion.16 = bf16[1,448,2048]{2,1,0:T(8,128)(2,1)} fusion(bf16[1024,448]{1,0:T(8,128)(2,1)S(1)} %bitcast.73, bf16[1024,6144]{1,0:T(8,128)(2,1)} %all-gather.2.cloned.1.call-done), kind=kOutput, calls=%fused_computation.17 | convolution fusion | flops 1880883200 | bytes 6946816 | tf_op jit(solution)/shard_map/dot_general | solution.py:101
  350.6 12.0 %all-to-all-done.4 = bf16[16,64,448]{2,1,0:T(8,128)(2,1)} async-done(((bf16[16,64,448]{2,1,0:T(8,128)(2,1)}), bf16[16,64,448]{2,1,0:T(8,128)(2,1)}, u32[]{:S(2)}, u32[]{:S(2)}) %all-to-all-start.4) | async-done | bytes 917536 | tf_op jit(solution)/shard_map/all_to_all | solution.py:91
  362.7 4.1 %all-to-all-start.5 = ((bf16[8,2,64,448]{3,2,1,0:T(8,128)(2,1)}), bf16[8,2,64,448]{3,2,1,0:T(8,128)(2,1)S(1)}, u32[]{:S(2)}, u32[]{:S(2)}) async-start(bf16[8,2,64,448]{3,2,1,0:T(8,128)(2,1)} %bitcast.20), calls=%async_computation.6 | async-start | bytes 2097152 | tf_op jit(solution)/shard_map/all_to_all | solution.py:94
  366.8 5.8 %fusion.19 = bf16[1,448,2048]{2,1,0:T(8,128)(2,1)} fusion(bf16[1024,448]{1,0:T(8,128)(2,1)} %bitcast.71, bf16[1024,6144]{1,0:T(8,128)(2,1)} %all-gather.2.cloned.1.call-done), kind=kOutput, calls=%fused_computation.18 | convolution fusion | flops 1880883200 | bytes 7077888 | tf_op jit(solution)/shard_map/dot_general | solution.py:102
  372.6 5.9 %fusion.22 = bf16[1,2048,448]{1,2,0:T(8,128)(2,1)} fusion(bf16[1024,448]{1,0:T(8,128)(2,1)} %bitcast.17, bf16[1024,6144]{1,0:T(8,128)(2,1)} %all-gather.2.cloned.1.call-done), kind=kOutput, calls=%fused_computation.19 | convolution fusion | flops 1880883200 | bytes 7077888 | tf_op jit(solution)/shard_map/dot_general | solution.py:103
  378.4 4.1 %all-to-all-done.5 = bf16[8,2,64,448]{3,2,1,0:T(8,128)(2,1)S(1)} async-done(((bf16[8,2,64,448]{3,2,1,0:T(8,128)(2,1)}), bf16[8,2,64,448]{3,2,1,0:T(8,128)(2,1)S(1)}, u32[]{:S(2)}, u32[]{:S(2)}) %all-to-all-start.5) | async-done | bytes 917536 | tf_op jit(solution)/shard_map/all_to_all | solution.py:94
  (49 shorter events, 14.9 us)
Async XLA Ops:
  7.2 77.9 %copy-start = (bf16[1,448,2048]{2,1,0:T(8,128)(2,1)S(1)}, bf16[1,448,2048]{2,1,0:T(8,128)(2,1)}, u32[]{:S(2)}) copy-start(bf16[1,448,2048]{2,1,0:T(8,128)(2,1)} %param.12) | copy-start | bytes 5505028
  11.4 7.6 %copy-start.4 = (bf16[128,896]{1,0:T(8,128)(2,1)S(1)}, bf16[128,896]{1,0:T(8,128)(2,1)}, u32[]{:S(2)}) copy-start(bf16[128,896]{1,0:T(8,128)(2,1)} %param.8) | copy-start | bytes 688132
  12.6 22.2 %all-to-all-start = ((bf16[8,2,64,448]{3,2,1,0:T(8,128)(2,1)}), bf16[8,2,64,448]{3,2,1,0:T(8,128)(2,1)S(1)}, u32[]{:S(2)}, u32[]{:S(2)}) async-start(bf16[8,2,64,448]{3,2,1,0:T(8,128)(2,1)} %copy.31), calls=%async_computation | async-start | bytes 2097152 | tf_op jit(solution)/shard_map/all_to_all | solution.py:57
  79.9 22.7 %all-to-all-start.3 = ((bf16[16,64,448]{2,1,0:T(8,128)(2,1)}), bf16[16,64,448]{2,1,0:T(8,128)(2,1)}, u32[]{:S(2)}, u32[]{:S(2)}) async-start(bf16[16,64,448]{2,1,0:T(8,128)(2,1)} %bitcast.63), calls=%async_computation.3 | async-start | bytes 2097152 | tf_op jit(solution)/shard_map/all_to_all | solution.py:60
  85.0 150.0 %reduce-scatter.2.cloned.1.call-start = ((), (), s32[]{:S(2)}) async-start(), calls=%async_computation.7 | async-start | bytes 13369344 | tf_op jit(solution)/shard_map/reduce_scatter | solution.py:69
  85.1 5.7 %copy-start.3 = (bf16[16,64,448]{2,1,0:T(8,128)(2,1)S(1)}, bf16[16,64,448]{2,1,0:T(8,128)(2,1)}, u32[]{:S(2)}) copy-start(bf16[16,64,448]{2,1,0:T(8,128)(2,1)} %all_to_all.31) | copy-start | bytes 2752516
  85.1 5.7 %copy-start.6 = (bf16[1,448,2048]{2,1,0:T(8,128)(2,1)S(1)}, bf16[1,448,2048]{2,1,0:T(8,128)(2,1)}, u32[]{:S(2)}) copy-start(bf16[1,448,2048]{2,1,0:T(8,128)(2,1)} %param.11) | copy-start | bytes 5505028
  102.6 4.3 %copy-start.1 = (bf16[1024,2048]{1,0:T(8,128)(2,1)S(1)}, bf16[1024,2048]{1,0:T(8,128)(2,1)}, u32[]{:S(2)}) copy-start(bf16[1024,2048]{1,0:T(8,128)(2,1)} %convolution_convert_fusion.1) | copy-start | bytes 12582916
  102.6 4.3 %copy-start.2 = (bf16[1024,2048]{1,0:T(8,128)(2,1)S(1)}, bf16[1024,2048]{1,0:T(8,128)(2,1)}, u32[]{:S(2)}) copy-start(bf16[1024,2048]{1,0:T(8,128)(2,1)} %convolution_convert_fusion.2) | copy-start | bytes 12582916
  118.4 0.7 copy-start.5
  118.4 210.4 %all-gather.2.cloned.1.call-start = ((), (), s32[]{:S(2)}) async-start(), calls=%async_computation.8 | async-start | bytes 13369344 | tf_op jit(solution)/shard_map/all_gather | solution.py:83
  328.8 4.4 %copy-start.7 = (bf16[1,448,2048]{2,1,0:T(8,128)(2,1)S(1)}, bf16[1,448,2048]{2,1,0:T(8,128)(2,1)}, u32[]{:S(2)}) copy-start(bf16[1,448,2048]{2,1,0:T(8,128)(2,1)} %param.11) | copy-start | bytes 5505028
  340.8 21.9 %all-to-all-start.4 = ((bf16[16,64,448]{2,1,0:T(8,128)(2,1)}), bf16[16,64,448]{2,1,0:T(8,128)(2,1)}, u32[]{:S(2)}, u32[]{:S(2)}) async-start(bf16[16,64,448]{2,1,0:T(8,128)(2,1)} %bitcast.19), calls=%async_computation.5 | async-start | bytes 2097152 | tf_op jit(solution)/shard_map/all_to_all | solution.py:91
  362.7 19.9 %all-to-all-start.5 = ((bf16[8,2,64,448]{3,2,1,0:T(8,128)(2,1)}), bf16[8,2,64,448]{3,2,1,0:T(8,128)(2,1)S(1)}, u32[]{:S(2)}, u32[]{:S(2)}) async-start(bf16[8,2,64,448]{3,2,1,0:T(8,128)(2,1)} %bitcast.20), calls=%async_computation.6 | async-start | bytes 2097152 | tf_op jit(solution)/shard_map/all_to_all | solution.py:94
Sparse Core Ops, SparseCore 0:
  118.5 116.5 reduce-scatter.1
  238.4 90.3 all-gather.1

commit v2 on v1

v2 whole, which is shorter than its diff:
```python
import functools
import math

import jax
import jax.numpy as jnp
from jax import lax
from jax.experimental import pallas as pl
from jax.experimental.pallas import tpu as pltpu
from jax.sharding import PartitionSpec as P

MESH = pl.DeviceIdType.MESH
CHUNKS = 8
X_WAYS, Z_WAYS, CORES = 4, 2, 2
LAST = (((1,), (1,)), ((), ()))
SUM_ORDER = "zxzzxzzx"
SPREAD_ORDER = "xzxxzxxz"


class Place:
    def __init__(self):
        self.expert = lax.axis_index("expert")
        d = lax.axis_index("dp")
        self.c = d % CORES
        self.x = (d // CORES) % X_WAYS
        self.zh = d // (CORES * X_WAYS)

    def at(self, zh, x, c):
        return (self.expert, (zh * X_WAYS + x) * CORES + c)

    def partner(self):
        return self.at(self.zh, self.x, 1 - self.c)

    def opposite(self):
        return self.at(1 - self.zh, self.x, self.c)

    def along_x(self, k):
        return (self.x + k) % X_WAYS

    def ring(self, k):
        return self.at(self.zh, self.along_x(k), self.c)

    def greet(self):
        barrier = pltpu.get_barrier_semaphore()
        peers = [self.partner(), self.opposite()] + [self.ring(k) for k in range(1, X_WAYS)]
        for peer in peers:
            pl.semaphore_signal(barrier, inc=1, device_id=peer, device_id_type=MESH)
        pl.semaphore_wait(barrier, len(peers))


def sum_kernel(
    x_ref, g_ref, wg_ref, wu_ref, wd_ref, pw_ref, out_ref,
    xp, gp, away, arrived, held, first, second, send_sem, recv_sem,
):
    me = Place()
    me.greet()
    n = wg_ref.shape[1] // CHUNKS
    blocks, rows = X_WAYS * Z_WAYS, x_ref.shape[2]

    for i in range(blocks):
        at = pl.ds(i * rows, rows)
        xp[0, at, :] = x_ref[i, me.c]
        xp[1, at, :] = x_ref[i, 1 - me.c]
        gp[0, at, :] = g_ref[i, me.c]
        gp[1, at, :] = g_ref[i, 1 - me.c]

    def copy(j, lane, src, dst, peer):
        return pltpu.make_async_remote_copy(
            src_ref=src, dst_ref=dst, send_sem=send_sem.at[j, lane], recv_sem=recv_sem.at[j, lane],
            device_id=peer, device_id_type=MESH,
        )

    def products(j, which, dst):
        cols = pl.ds(j * n, n)
        parts = (
            jnp.dot(xp[which], wg_ref[:, cols], preferred_element_type=jnp.float32),
            jnp.dot(xp[which], wu_ref[:, cols], preferred_element_type=jnp.float32),
            lax.dot_general(gp[which], wd_ref[cols, :], LAST, preferred_element_type=jnp.float32),
        )
        for k, part in enumerate(parts):
            dst[j, :, :, :, k * n : (k + 1) * n] = part.astype(jnp.bfloat16).reshape(
                Z_WAYS, X_WAYS, rows, n
            )

    def to_partner(j):
        return copy(j, 0, away.at[j], arrived.at[j], me.partner())

    def first_copies(j):
        if SUM_ORDER[j] == "x":
            return [
                copy(j, k, held.at[j, :, me.along_x(k)], first.at[j, pl.ds(2 * (k - 1), 2)], me.ring(k))
                for k in range(1, X_WAYS)
            ]
        return [copy(j, 1, held.at[j, 1 - me.zh], first.at[j, pl.ds(0, X_WAYS)], me.opposite())]

    def second_copies(j):
        if SUM_ORDER[j] == "x":
            return [copy(j, 4, held.at[j, 1 - me.zh, me.x], second.at[j, 0], me.opposite())]
        return [
            copy(j, 3 + k, held.at[j, me.zh, me.along_x(k)], second.at[j, k - 1], me.ring(k))
            for k in range(1, X_WAYS)
        ]

    f32 = jnp.float32

    def stage0(j):
        products(j, 1, away)
        to_partner(j).start()
        products(j, 0, held)

    def stage1(j):
        to_partner(j).wait_recv()
        for z in range(Z_WAYS):
            held[j, z] = (held[j, z].astype(f32) + arrived[j, z].astype(f32)).astype(jnp.bfloat16)
        for one in first_copies(j):
            one.start()

    def stage2(j):
        for one in first_copies(j):
            one.wait_recv()
        if SUM_ORDER[j] == "x":
            for z in range(Z_WAYS):
                total = held[j, z, me.x].astype(f32)
                for k in range(X_WAYS - 1):
                    total += first[j, 2 * k + z].astype(f32)
                held[j, z, me.x] = total.astype(jnp.bfloat16)
        else:
            for x in range(X_WAYS):
                held[j, me.zh, x] = (held[j, me.zh, x].astype(f32) + first[j, x].astype(f32)).astype(
                    jnp.bfloat16
                )
        for one in second_copies(j):
            one.start()

    def stage3(j):
        for one in second_copies(j):
            one.wait_recv()
        total = held[j, me.zh, me.x].astype(f32)
        for k in range(1 if SUM_ORDER[j] == "x" else X_WAYS - 1):
            total += second[j, k].astype(f32)
        weight = pw_ref[...]
        gate, upper, back = total[:, :n], total[:, n : 2 * n], total[:, 2 * n :] * weight
        s = 1.0 / (1.0 + jnp.exp(-gate))
        out_ref[j, :, :n] = (weight * gate * s * upper).astype(jnp.bfloat16)
        out_ref[j, :, n : 2 * n] = (back * upper * s * (1.0 + gate * (1.0 - s))).astype(jnp.bfloat16)
        out_ref[j, :, 2 * n :] = (back * gate * s).astype(jnp.bfloat16)

    stages = (stage0, stage1, stage2, stage3)
    lags = (0, 1, 3, 5)
    for t in range(CHUNKS + lags[-1]):
        for stage, lag in zip(stages, lags):
            if 0 <= t - lag < CHUNKS:
                stage(t - lag)
    for j in range(CHUNKS):
        for one in [to_partner(j)] + first_copies(j) + second_copies(j):
            one.wait_send()


def spread_kernel(
    inv_root, act_ref, x_ref, g_ref, wg_ref, wu_ref, gg_ref, gu_ref, gd_ref, dx_ref,
    xt, gt, whole, total, send_sem, recv_sem,
):
    me = Place()
    me.greet()
    n = wg_ref.shape[1] // CHUNKS
    blocks, rows = X_WAYS * Z_WAYS, x_ref.shape[2]
    slots = CORES * blocks * rows
    f32 = jnp.float32

    def copy(j, lane, src, dst, peer):
        return pltpu.make_async_remote_copy(
            src_ref=src, dst_ref=dst, send_sem=send_sem.at[j, lane], recv_sem=recv_sem.at[j, lane],
            device_id=peer, device_id_type=MESH,
        )

    def first_copies(j):
        if SPREAD_ORDER[j] == "x":
            return [
                copy(j, k, act_ref.at[j], whole.at[j, 0, me.zh, me.x], me.ring(k))
                for k in range(1, X_WAYS)
            ]
        return [copy(j, 1, act_ref.at[j], whole.at[j, 0, me.zh, me.x], me.opposite())]

    def second_copies(j):
        if SPREAD_ORDER[j] == "x":
            return [copy(j, 4, whole.at[j, 0, me.zh], whole.at[j, 0, me.zh], me.opposite())]
        return [
            copy(j, 3 + k, whole.at[j, 0, :, me.x], whole.at[j, 0, :, me.x], me.ring(k))
            for k in range(1, X_WAYS)
        ]

    def to_partner(j):
        return copy(j, 0, whole.at[j, 0], whole.at[j, 1], me.partner())

    def stage0(j):
        for one in first_copies(j):
            one.start()
        whole[j, 0, me.zh, me.x] = act_ref[j]

    def stage1(j):
        for one in first_copies(j):
            one.wait_recv()
        for one in second_copies(j):
            one.start()

    def stage2(j):
        for one in second_copies(j):
            one.wait_recv()
        to_partner(j).start()

    def stage3(j):
        to_partner(j).wait_recv()
        cols = pl.ds(j * n, n)
        scaled = whole[j, :, :, :, :, :n].reshape(slots, n)
        d_gate = whole[j, :, :, :, :, n : 2 * n].reshape(slots, n)
        d_up = whole[j, :, :, :, :, 2 * n :].reshape(slots, n)
        part = lax.dot_general(d_gate, wg_ref[:, cols], LAST, preferred_element_type=f32)
        part += lax.dot_general(d_up, wu_ref[:, cols], LAST, preferred_element_type=f32)
        total[...] = part if j == 0 else total[...] + part
        gg_ref[:, cols] = (jnp.dot(xt[...], d_gate, preferred_element_type=f32) * inv_root).astype(jnp.bfloat16)
        gu_ref[:, cols] = (jnp.dot(xt[...], d_up, preferred_element_type=f32) * inv_root).astype(jnp.bfloat16)
        down = jnp.dot(gt[...], scaled, preferred_element_type=f32) * inv_root
        gd_ref[cols, :] = down.T.astype(jnp.bfloat16)

    for j in range(CHUNKS):
        stage0(j)
    for i in range(blocks):
        for which in range(CORES):
            c = me.c if which == 0 else 1 - me.c
            at = pl.ds((which * blocks + i) * rows, rows)
            total[at, :] = x_ref[i, c].astype(f32)
    xt[...] = total[...].T.astype(jnp.bfloat16)
    for i in range(blocks):
        for which in range(CORES):
            c = me.c if which == 0 else 1 - me.c
            at = pl.ds((which * blocks + i) * rows, rows)
            total[at, :] = g_ref[i, c].astype(f32)
    gt[...] = total[...].T.astype(jnp.bfloat16)
    stages = (stage1, stage2, stage3)
    lags = (0, 2, 3)
    for t in range(CHUNKS + lags[-1]):
        for stage, lag in zip(stages, lags):
            if 0 <= t - lag < CHUNKS:
                stage(t - lag)
    for i in range(blocks):
        for which in range(CORES):
            c = me.c if which == 0 else 1 - me.c
            at = pl.ds((which * blocks + i) * rows, rows)
            dx_ref[i, c] = total[at, :].astype(jnp.bfloat16)
    for j in range(CHUNKS):
        for one in [to_partner(j)] + first_copies(j) + second_copies(j):
            one.wait_send()


def vmem(count):
    return [pl.BlockSpec(memory_space=pltpu.VMEM)] * count


def summed_rows(x, g, w_gate, w_up, w_down, weight):
    (blocks, cores, rows, shard), hidden = x.shape, w_gate.shape[1]
    cols = 3 * hidden // CHUNKS
    bf16 = jnp.bfloat16
    return pl.pallas_call(
        sum_kernel,
        out_shape=jax.ShapeDtypeStruct((CHUNKS, rows, cols), bf16),
        in_specs=vmem(6),
        out_specs=vmem(1)[0],
        scratch_shapes=[
            pltpu.VMEM((cores, blocks * rows, shard), bf16),
            pltpu.VMEM((cores, blocks * rows, shard), bf16),
            pltpu.VMEM((CHUNKS, Z_WAYS, X_WAYS, rows, cols), bf16),
            pltpu.VMEM((CHUNKS, Z_WAYS, X_WAYS, rows, cols), bf16),
            pltpu.VMEM((CHUNKS, Z_WAYS, X_WAYS, rows, cols), bf16),
            pltpu.VMEM((CHUNKS, 2 * (X_WAYS - 1), rows, cols), bf16),
            pltpu.VMEM((CHUNKS, X_WAYS - 1, rows, cols), bf16),
            pltpu.SemaphoreType.DMA((CHUNKS, 7)),
            pltpu.SemaphoreType.DMA((CHUNKS, 7)),
        ],
        compiler_params=pltpu.CompilerParams(
            collective_id=0, has_side_effects=True, vmem_limit_bytes=50 << 20
        ),
    )(x, g, w_gate, w_up, w_down, weight)


def spread_rows(inv_root, act, x, g, w_gate, w_up):
    (blocks, cores, rows, shard), hidden = x.shape, w_gate.shape[1]
    cols = 3 * hidden // CHUNKS
    slots = cores * blocks * rows
    bf16 = jnp.bfloat16
    return pl.pallas_call(
        functools.partial(spread_kernel, inv_root),
        out_shape=(
            jax.ShapeDtypeStruct((shard, hidden), bf16),
            jax.ShapeDtypeStruct((shard, hidden), bf16),
            jax.ShapeDtypeStruct((hidden, shard), bf16),
            jax.ShapeDtypeStruct(x.shape, bf16),
        ),
        in_specs=vmem(5),
        out_specs=vmem(4),
        scratch_shapes=[
            pltpu.VMEM((shard, slots), bf16),
            pltpu.VMEM((shard, slots), bf16),
            pltpu.VMEM((CHUNKS, cores, Z_WAYS, X_WAYS, rows, cols), bf16),
            pltpu.VMEM((slots, shard), jnp.float32),
            pltpu.SemaphoreType.DMA((CHUNKS, 7)),
            pltpu.SemaphoreType.DMA((CHUNKS, 7)),
        ],
        compiler_params=pltpu.CompilerParams(
            collective_id=1, has_side_effects=True, vmem_limit_bytes=50 << 20
        ),
    )(act, x, g, w_gate, w_up)


def body(tokens, grad_out, expert_ids, route_weights, w_gate, w_up, w_down):
    experts = lax.axis_size("expert")
    groups = lax.axis_size("dp")
    tok_rows, width = tokens.shape
    capacity = tok_rows // 2
    expert_index = lax.axis_index("expert")
    inv_root = 1.0 / math.sqrt(tok_rows * groups)
    rows_first = (((0,), (0,)), ((), ()))
    gate_shard, up_shard, down_shard = w_gate[0], w_up[0], w_down[0]
    shard = gate_shard.shape[0]
    halves = width // shard

    names = jnp.arange(experts, dtype=jnp.int32)[:, None]
    hit0 = expert_ids[:, 0][None, :] == names
    hit1 = expert_ids[:, 1][None, :] == names
    hit = (hit0 | hit1).astype(jnp.bfloat16)
    index = jnp.arange(tok_rows, dtype=jnp.int32)
    before = (index[:, None] < index[None, :]).astype(jnp.bfloat16)
    rank = jnp.dot(hit, before, preferred_element_type=jnp.float32)
    rank = jnp.where(hit > 0, rank, -1.0).astype(jnp.int32)
    chosen = rank[:, None, :] == jnp.arange(capacity, dtype=jnp.int32)[None, :, None]
    dispatch = chosen.astype(jnp.bfloat16).reshape(experts * capacity, tok_rows)
    weight_of = jnp.where(hit0, route_weights[:, 0][None, :], 0.0) + jnp.where(
        hit1, route_weights[:, 1][None, :], 0.0
    )
    own_rank = lax.dynamic_slice_in_dim(rank, expert_index, 1)
    own_weight_of = lax.dynamic_slice_in_dim(weight_of, expert_index, 1)
    own_weight = jnp.sum(
        jnp.where(
            own_rank == jnp.arange(capacity, dtype=jnp.int32)[:, None], own_weight_of, 0.0
        ),
        axis=1,
    )

    def send(rows):
        picked = [
            jnp.dot(
                dispatch,
                rows[:, h * shard : (h + 1) * shard],
                preferred_element_type=jnp.float32,
            )
            .astype(jnp.bfloat16)
            .reshape(experts, 1, capacity, shard)
            for h in range(halves)
        ]
        moved = lax.all_to_all(
            jnp.concatenate(picked, axis=1), "expert", split_axis=0, concat_axis=0, tiled=True
        )
        return lax.all_to_all(
            moved.reshape(groups, capacity, shard), "dp", split_axis=0, concat_axis=0, tiled=True
        ).reshape(groups // CORES, CORES, capacity, shard)

    x_block = send(tokens)
    g_block = send(grad_out)
    act = summed_rows(x_block, g_block, gate_shard, up_shard, down_shard, own_weight[:, None])
    grad_g, grad_u, grad_d, dx_rows = spread_rows(
        inv_root, act, x_block, g_block, gate_shard, up_shard
    )
    returned = lax.all_to_all(
        dx_rows.reshape(groups, capacity, shard), "dp", split_axis=0, concat_axis=0, tiled=True
    )
    returned = lax.all_to_all(
        returned.reshape(experts, halves, capacity, shard),
        "expert",
        split_axis=0,
        concat_axis=0,
        tiled=True,
    )
    grad_tokens = jnp.concatenate(
        [
            lax.dot_general(
                dispatch,
                returned[:, h].reshape(experts * capacity, shard),
                rows_first,
                preferred_element_type=jnp.float32,
            ).astype(jnp.bfloat16)
            for h in range(halves)
        ],
        axis=1,
    )
    return (grad_tokens, grad_g[None], grad_u[None], grad_d[None])


def solution(mesh):
    in_specs = (
        P("dp", "expert"),
        P("dp", "expert"),
        P("dp", None),
        P("dp", None),
        P("expert", "dp", None),
        P("expert", "dp", None),
        P("expert", None, "dp"),
    )
    out_specs = (
        P("dp", "expert"),
        P("expert", "dp", None),
        P("expert", "dp", None),
        P("expert", None, "dp"),
    )
    return jax.shard_map(body, mesh=mesh, in_specs=in_specs, out_specs=out_specs, check_vma=False)
```

time: 392 us -> 272 us (0.69)
  waiting for transfers between devices: 238 us -> 41.2 us
  Pallas kernels: 0 us -> 131 us
  matrix products: 47.8 us -> 4.06 us
  blocking collectives: 45.1 us -> 65.6 us
  other arithmetic: 15.6 us -> 0.56 us
  between operations: 14.2 us -> 0.85 us
  starting transfers between devices: 20.2 us -> 14.5 us
    pallas_call x0 -> x2, Pallas kernels: none -> 131 us  [the longest x1 70.2 us: spread_rows(): pl.pallas_call(functools.partial(spread_kernel, inv_root), out_shape=(jax...]
    reduce_scatter x1 -> x0, waiting for transfers between devices: 116 us -> none  [body(): lax.psum_scatter(jnp.concatenate([gate, upper, back], axis=1).astype(jnp....]
    all_gather x1 -> x0, waiting for transfers between devices: 91.2 us -> none  [body(): piece = lax.all_gather(local, 'dp', axis=0, tiled=True)]
    dot_general x8 -> x0, matrix products: 41.2 us -> none  [the longest x1 5.85 us: body(): lax.dot_general(scaled, g_block, rows_first, preferred_element_type=jnp.f...]
    all_to_all x0 -> x1, blocking collectives: none -> 21.6 us  [body(): lax.all_to_all(dx_rows.reshape(groups, capacity, shard), 'dp', split_axis...]
    concatenate x2 -> x0, other arithmetic: 12.4 us -> none  [the longest x1 11.4 us: body(): jnp.concatenate([gate, upper, back], axis=1).astype(jnp.bfloat16)]
    all_to_all x1 -> x0, waiting for transfers between devices: 12 us -> none  [body(): lax.all_to_all(dx_rows.reshape(groups, capacity, shard), 'dp', split_axis...]
    all_to_all x1, waiting for transfers between devices: 4.11 us -> 13.4 us  [body(): lax.all_to_all(returned.reshape(experts, halves, capacity, shard), 'exper...]
  transfers between devices with their start and end apart: 6 -> 3, of which waited for: 6 -> 3; matrix products, arithmetic and copies ran while one was open for 9% -> 3% of each run, Pallas kernels for 0% -> 0%
where the time goes in v2:
time: 272 us; the launch traced here: 271 us
  Pallas kernels  131 us (48%)
  blocking collectives  65.6 us (24%)
  waiting for transfers between devices  41.2 us (15%)
  starting transfers between devices  14.5 us (5%)
  local copies, waits for them, and re-layouts  13.4 us (5%)
  matrix products  4.06 us (1%)
    pallas_call x1, Pallas kernels, spread_rows(): pl.pallas_call(functools.partial(spread_kernel, inv_root), out_shape=(jax...  70.2 us
    pallas_call x1, Pallas kernels, summed_rows(): pl.pallas_call(sum_kernel, out_shape=jax.ShapeDtypeStruct((CHUNKS, rows,...  61.2 us
    all_to_all x1, blocking collectives, send(): lax.all_to_all(moved.reshape(groups, capacity, shard), 'dp', split_axis=0...  26.1 us
    all_to_all x1, blocking collectives, body(): lax.all_to_all(dx_rows.reshape(groups, capacity, shard), 'dp', split_axis...  21.6 us
    all_to_all x1, blocking collectives, send(): lax.all_to_all(jnp.concatenate(picked, axis=1), 'expert', split_axis=0, c...  17.9 us
    all_to_all x1, waiting for transfers between devices, send(): lax.all_to_all(jnp.concatenate(picked, axis=1), 'expert', split_axis=0, c...  14.4 us
    all_to_all x1, waiting for transfers between devices, body(): lax.all_to_all(returned.reshape(experts, halves, capacity, shard), 'exper...  13.4 us
    all_to_all x1, waiting for transfers between devices, send(): lax.all_to_all(moved.reshape(groups, capacity, shard), 'dp', split_axis=0...  13.4 us
  transfers between devices with their start and end apart: 3, of which 3 were waited for; matrix products, arithmetic and copies ran while one was open for 3% of the time, Pallas kernels for 0%

profile of v2, /device:TPU:1, one launch (start us, length us, event | category | flops | bytes accessed | tf_op | source)
XLA Modules:
  0.0 271.4 jit_solution(14924924924764975642)
XLA Ops:
  0.6 0.8 slice_bitcast_fusion.3
  1.8 1.2 convolution_convert_fusion.1
  3.0 1.3 convolution_convert_fusion
  4.9 1.1 copy.50
  5.9 6.4 %all-to-all-start.2 = ((bf16[8,2,64,448]{3,2,1,0:T(8,128)(2,1)}), bf16[8,2,64,448]{3,2,1,0:T(8,128)(2,1)S(1)}, u32[]{:S(2)}, u32[]{:S(2)}) async-start(bf16[8,2,64,448]{3,2,1,0:T(8,128)(2,1)} %copy.50), calls=%async_computation.2 | async-start | bytes 2097152 | tf_op jit(solution)/shard_map/all_to_all | solution.py:358
  12.9 0.4 convolution_convert_fusion.2
  13.7 14.4 %all-to-all-done.2 = bf16[8,2,64,448]{3,2,1,0:T(8,128)(2,1)S(1)} async-done(((bf16[8,2,64,448]{3,2,1,0:T(8,128)(2,1)}), bf16[8,2,64,448]{3,2,1,0:T(8,128)(2,1)S(1)}, u32[]{:S(2)}, u32[]{:S(2)}) %all-to-all-start.2) | async-done | bytes 917536 | tf_op jit(solution)/shard_map/all_to_all | solution.py:358
  28.1 17.9 %all_to_all.30 = bf16[8,2,64,448]{3,2,1,0:T(8,128)(2,1)} all-to-all(bf16[8,2,64,448]{3,2,1,0:T(8,128)(2,1)S(1)} %copy.47), channel_id=1, replica_groups=mesh['expert'=8,'dp'=16] {'expert'}, dimensions={0} | all-to-all | bytes 1835008 | tf_op jit(solution)/shard_map/all_to_all | solution.py:358
  46.1 26.1 %all_to_all.31 = bf16[16,64,448]{2,1,0:T(8,128)(2,1)S(1)} all-to-all(bf16[16,64,448]{2,1,0:T(8,128)(2,1)S(1)} %bitcast.52), channel_id=1, replica_groups=mesh['expert'=8,'dp'=16] {'dp'}, dimensions={0} | all-to-all | bytes 1835008 | tf_op jit(solution)/shard_map/all_to_all | solution.py:361
  72.1 4.5 %all-to-all-start.1 = ((bf16[16,64,448]{2,1,0:T(8,128)(2,1)}), bf16[16,64,448]{2,1,0:T(8,128)(2,1)S(1)}, u32[]{:S(2)}, u32[]{:S(2)}) async-start(bf16[16,64,448]{2,1,0:T(8,128)(2,1)} %bitcast.6), calls=%async_computation.1 | async-start | bytes 2097152 | tf_op jit(solution)/shard_map/all_to_all | solution.py:361
  76.9 3.8 %copy.51 = bf16[1,2048,448]{2,1,0:T(8,128)(2,1)} copy(bf16[1,2048,448]{1,2,0:T(8,128)(2,1)} %param.13) | data formatting | bytes 3670016 | tf_op args[6]
  80.7 13.4 %all-to-all-done.1 = bf16[16,64,448]{2,1,0:T(8,128)(2,1)S(1)} async-done(((bf16[16,64,448]{2,1,0:T(8,128)(2,1)}), bf16[16,64,448]{2,1,0:T(8,128)(2,1)S(1)}, u32[]{:S(2)}, u32[]{:S(2)}) %all-to-all-start.1) | async-done | bytes 917536 | tf_op jit(solution)/shard_map/all_to_all | solution.py:361
  94.1 61.2 %shard_map.102.act_ref = bf16[8,64,768]{2,1,0:T(8,128)(2,1)S(1)} custom-call(bf16[8,2,64,448]{3,2,1,0:T(8,128)(2,1)S(1)} %bitcast.44, bf16[8,2,64,448]{3,2,1,0:T(8,128)(2,1)S(1)} %bitcast.42, bf16[448,2048]{1,0:T(8,128)(2,1)} %bitcast.48, bf16[448,2048]{1,0:T(8,128)(2,1)} %bitcast.50, bf16[2048,448]{1,0:T(8,128)(2,1)} %bitcast.47, f32[64,1]{1,0:T(8,128)S(1)} %copy.52.pw_ref), custom_call_target="tpu_custom_call" | custom-call | tf_op jit(solution)/shard_map/pallas_call | solution.py:262
  155.3 70.2 %shard_map.103 = (bf16[448,2048]{1,0:T(8,128)(2,1)}, bf16[448,2048]{1,0:T(8,128)(2,1)}, bf16[2048,448]{1,0:T(8,128)(2,1)}, bf16[8,2,64,448]{3,2,1,0:T(8,128)(2,1)S(1)}) custom-call(bf16[8,64,768]{2,1,0:T(8,128)(2,1)S(1)} %shard_map.102.act_ref, bf16[8,2,64,448]{3,2,1,0:T(8,128)(2,1)S(1)} %bitcast.45, bf16[8,2,64,448]{3,2,1,0:T(8,128)(2,1)S(1)} %bitcast.43, ...), custom_call_target="tpu_custom_call" | custom-call | tf_op jit(solution)/shard_map/pallas_call | solution.py:289
  225.5 21.6 %all_to_all.32 = bf16[16,64,448]{2,1,0:T(8,128)(2,1)} all-to-all(bf16[16,64,448]{2,1,0:T(8,128)(2,1)S(1)} %bitcast.46), channel_id=1, replica_groups=mesh['expert'=8,'dp'=16] {'dp'}, dimensions={0} | all-to-all | bytes 1835008 | tf_op jit(solution)/shard_map/all_to_all | solution.py:371
  247.1 3.6 %all-to-all-start.5 = ((bf16[8,2,64,448]{3,2,1,0:T(8,128)(2,1)}), bf16[8,2,64,448]{3,2,1,0:T(8,128)(2,1)S(1)}, u32[]{:S(2)}, u32[]{:S(2)}) async-start(bf16[8,2,64,448]{3,2,1,0:T(8,128)(2,1)} %bitcast.21), calls=%async_computation.5 | async-start | bytes 2097152 | tf_op jit(solution)/shard_map/all_to_all | solution.py:374
  250.7 2.3 copy.54
  253.0 13.4 %all-to-all-done.5 = bf16[8,2,64,448]{3,2,1,0:T(8,128)(2,1)S(1)} async-done(((bf16[8,2,64,448]{3,2,1,0:T(8,128)(2,1)}), bf16[8,2,64,448]{3,2,1,0:T(8,128)(2,1)S(1)}, u32[]{:S(2)}, u32[]{:S(2)}) %all-to-all-start.5) | async-done | bytes 917536 | tf_op jit(solution)/shard_map/all_to_all | solution.py:374
  266.5 0.3 convolution_convert_fusion.5
  266.8 0.3 convolution_convert_fusion.4
  267.2 0.8 copy.53
  268.0 1.2 copy.65
  269.3 0.9 copy-done.1
  270.2 1.2 copy.66
  (30 shorter events, 2.2 us)
Async XLA Ops:
  4.8 7.5 %copy-start.3 = (bf16[128,896]{1,0:T(8,128)(2,1)S(1)}, bf16[128,896]{1,0:T(8,128)(2,1)}, u32[]{:S(2)}) copy-start(bf16[128,896]{1,0:T(8,128)(2,1)} %param.7) | copy-start | bytes 688132
  5.9 22.2 %all-to-all-start.2 = ((bf16[8,2,64,448]{3,2,1,0:T(8,128)(2,1)}), bf16[8,2,64,448]{3,2,1,0:T(8,128)(2,1)S(1)}, u32[]{:S(2)}, u32[]{:S(2)}) async-start(bf16[8,2,64,448]{3,2,1,0:T(8,128)(2,1)} %copy.50), calls=%async_computation.2 | async-start | bytes 2097152 | tf_op jit(solution)/shard_map/all_to_all | solution.py:358
  46.1 30.6 %copy-start.4 = (f32[128,2]{0,1:T(2,128)S(1)}, f32[128,2]{0,1:T(2,128)}, u32[]{:S(2)}) copy-start(f32[128,2]{0,1:T(2,128)} %param.10) | copy-start | bytes 3076
  72.1 22.0 %all-to-all-start.1 = ((bf16[16,64,448]{2,1,0:T(8,128)(2,1)}), bf16[16,64,448]{2,1,0:T(8,128)(2,1)S(1)}, u32[]{:S(2)}, u32[]{:S(2)}) async-start(bf16[16,64,448]{2,1,0:T(8,128)(2,1)} %bitcast.6), calls=%async_computation.1 | async-start | bytes 2097152 | tf_op jit(solution)/shard_map/all_to_all | solution.py:361
  225.5 25.2 %copy-start = (bf16[2048,448]{1,0:T(8,128)(2,1)S(1)}, bf16[2048,448]{1,0:T(8,128)(2,1)}, u32[]{:S(2)}) copy-start(bf16[2048,448]{1,0:T(8,128)(2,1)} %get-tuple-element.11) | copy-start | bytes 5505028
  247.1 19.3 %all-to-all-start.5 = ((bf16[8,2,64,448]{3,2,1,0:T(8,128)(2,1)}), bf16[8,2,64,448]{3,2,1,0:T(8,128)(2,1)S(1)}, u32[]{:S(2)}, u32[]{:S(2)}) async-start(bf16[8,2,64,448]{3,2,1,0:T(8,128)(2,1)} %bitcast.21), calls=%async_computation.5 | async-start | bytes 2097152 | tf_op jit(solution)/shard_map/all_to_all | solution.py:374
  253.0 15.0 %copy-start.2 = (bf16[448,2048]{1,0:T(8,128)(2,1)S(1)}, bf16[448,2048]{1,0:T(8,128)(2,1)}, u32[]{:S(2)}) copy-start(bf16[448,2048]{1,0:T(8,128)(2,1)} %get-tuple-element.9) | copy-start | bytes 5505028
  268.0 2.2 copy-start.1

commit v3 on v2

--- a/solution.py
+++ b/solution.py
@@ -48,20 +48,20 @@
 
 
 def sum_kernel(
-    x_ref, g_ref, wg_ref, wu_ref, wd_ref, pw_ref, out_ref,
+    rows_ref, wg_ref, wu_ref, wd_ref, pw_ref, out_ref,
     xp, gp, away, arrived, held, first, second, send_sem, recv_sem,
 ):
     me = Place()
     me.greet()
     n = wg_ref.shape[1] // CHUNKS
-    blocks, rows = X_WAYS * Z_WAYS, x_ref.shape[2]
+    blocks, rows, shard = X_WAYS * Z_WAYS, rows_ref.shape[2], wg_ref.shape[0]
 
     for i in range(blocks):
         at = pl.ds(i * rows, rows)
-        xp[0, at, :] = x_ref[i, me.c]
-        xp[1, at, :] = x_ref[i, 1 - me.c]
-        gp[0, at, :] = g_ref[i, me.c]
-        gp[1, at, :] = g_ref[i, 1 - me.c]
+        for which in range(CORES):
+            both = rows_ref[i, me.c if which == 0 else 1 - me.c]
+            xp[which, at, :] = both[:, :shard]
+            gp[which, at, :] = both[:, shard:]
 
     def copy(j, lane, src, dst, peer):
         return pltpu.make_async_remote_copy(
@@ -74,7 +74,7 @@
         parts = (
             jnp.dot(xp[which], wg_ref[:, cols], preferred_element_type=jnp.float32),
             jnp.dot(xp[which], wu_ref[:, cols], preferred_element_type=jnp.float32),
-            lax.dot_general(gp[which], wd_ref[cols, :], LAST, preferred_element_type=jnp.float32),
+            jnp.dot(gp[which], wd_ref[:, cols], preferred_element_type=jnp.float32),
         )
         for k, part in enumerate(parts):
             dst[j, :, :, :, k * n : (k + 1) * n] = part.astype(jnp.bfloat16).reshape(
@@ -156,13 +156,13 @@
 
 
 def spread_kernel(
-    inv_root, act_ref, x_ref, g_ref, wg_ref, wu_ref, gg_ref, gu_ref, gd_ref, dx_ref,
+    inv_root, act_ref, rows_ref, wg_ref, wu_ref, gg_ref, gu_ref, gd_ref, dx_ref,
     xt, gt, whole, total, send_sem, recv_sem,
 ):
     me = Place()
     me.greet()
     n = wg_ref.shape[1] // CHUNKS
-    blocks, rows = X_WAYS * Z_WAYS, x_ref.shape[2]
+    blocks, rows, shard = X_WAYS * Z_WAYS, rows_ref.shape[2], wg_ref.shape[0]
     slots = CORES * blocks * rows
     f32 = jnp.float32
 
@@ -218,23 +218,17 @@
         total[...] = part if j == 0 else total[...] + part
         gg_ref[:, cols] = (jnp.dot(xt[...], d_gate, preferred_element_type=f32) * inv_root).astype(jnp.bfloat16)
         gu_ref[:, cols] = (jnp.dot(xt[...], d_up, preferred_element_type=f32) * inv_root).astype(jnp.bfloat16)
-        down = jnp.dot(gt[...], scaled, preferred_element_type=f32) * inv_root
-        gd_ref[cols, :] = down.T.astype(jnp.bfloat16)
+        gd_ref[:, cols] = (jnp.dot(gt[...], scaled, preferred_element_type=f32) * inv_root).astype(jnp.bfloat16)
 
     for j in range(CHUNKS):
         stage0(j)
-    for i in range(blocks):
-        for which in range(CORES):
-            c = me.c if which == 0 else 1 - me.c
-            at = pl.ds((which * blocks + i) * rows, rows)
-            total[at, :] = x_ref[i, c].astype(f32)
-    xt[...] = total[...].T.astype(jnp.bfloat16)
-    for i in range(blocks):
-        for which in range(CORES):
-            c = me.c if which == 0 else 1 - me.c
-            at = pl.ds((which * blocks + i) * rows, rows)
-            total[at, :] = g_ref[i, c].astype(f32)
-    gt[...] = total[...].T.astype(jnp.bfloat16)
+    for lo, turned in ((0, xt), (shard, gt)):
+        for i in range(blocks):
+            for which in range(CORES):
+                c = me.c if which == 0 else 1 - me.c
+                at = pl.ds((which * blocks + i) * rows, rows)
+                total[at, :] = rows_ref[i, c][:, lo : lo + shard].astype(f32)
+        turned[...] = total[...].T.astype(jnp.bfloat16)
     stages = (stage1, stage2, stage3)
     lags = (0, 2, 3)
     for t in range(CHUNKS + lags[-1]):
@@ -245,7 +239,8 @@
         for which in range(CORES):
             c = me.c if which == 0 else 1 - me.c
             at = pl.ds((which * blocks + i) * rows, rows)
-            dx_ref[i, c] = total[at, :].astype(jnp.bfloat16)
+            done = total[at, :].astype(jnp.bfloat16)
+            dx_ref[i, c] = jnp.concatenate([done[: rows // 2], done[rows // 2 :]], axis=1)
     for j in range(CHUNKS):
         for one in [to_partner(j)] + first_copies(j) + second_copies(j):
             one.wait_send()
@@ -255,14 +250,14 @@
     return [pl.BlockSpec(memory_space=pltpu.VMEM)] * count
 
 
-def summed_rows(x, g, w_gate, w_up, w_down, weight):
-    (blocks, cores, rows, shard), hidden = x.shape, w_gate.shape[1]
+def summed_rows(packed, w_gate, w_up, w_down, weight):
+    (blocks, cores, rows, _), (shard, hidden) = packed.shape, w_gate.shape
     cols = 3 * hidden // CHUNKS
     bf16 = jnp.bfloat16
     return pl.pallas_call(
         sum_kernel,
         out_shape=jax.ShapeDtypeStruct((CHUNKS, rows, cols), bf16),
-        in_specs=vmem(6),
+        in_specs=vmem(5),
         out_specs=vmem(1)[0],
         scratch_shapes=[
             pltpu.VMEM((cores, blocks * rows, shard), bf16),
@@ -278,11 +273,11 @@
         compiler_params=pltpu.CompilerParams(
             collective_id=0, has_side_effects=True, vmem_limit_bytes=50 << 20
         ),
-    )(x, g, w_gate, w_up, w_down, weight)
-
-
-def spread_rows(inv_root, act, x, g, w_gate, w_up):
-    (blocks, cores, rows, shard), hidden = x.shape, w_gate.shape[1]
+    )(packed, w_gate, w_up, w_down, weight)
+
+
+def spread_rows(inv_root, act, packed, w_gate, w_up):
+    (blocks, cores, rows, width), (shard, hidden) = packed.shape, w_gate.shape
     cols = 3 * hidden // CHUNKS
     slots = cores * blocks * rows
     bf16 = jnp.bfloat16
@@ -291,10 +286,10 @@
         out_shape=(
             jax.ShapeDtypeStruct((shard, hidden), bf16),
             jax.ShapeDtypeStruct((shard, hidden), bf16),
-            jax.ShapeDtypeStruct((hidden, shard), bf16),
-            jax.ShapeDtypeStruct(x.shape, bf16),
+            jax.ShapeDtypeStruct((shard, hidden), bf16),
+            jax.ShapeDtypeStruct((blocks, cores, rows // 2, width), bf16),
         ),
-        in_specs=vmem(5),
+        in_specs=vmem(4),
         out_specs=vmem(4),
         scratch_shapes=[
             pltpu.VMEM((shard, slots), bf16),
@@ -307,20 +302,227 @@
         compiler_params=pltpu.CompilerParams(
             collective_id=1, has_side_effects=True, vmem_limit_bytes=50 << 20
         ),
-    )(act, x, g, w_gate, w_up)
+    )(act, packed, w_gate, w_up)
+
+
+FAR_DP = ((2, 1), (1, 1), (3, 1), (2, 0), (0, 1), (1, 0), (3, 0))
+FAR_EXPERT = ((2, 1), (1, 1), (3, 1), (2, 0), (1, 0), (3, 0), (0, 1))
+Y_WAYS, PAIR = 4, 2
+
+
+class Wide(Place):
+    def __init__(self):
+        super().__init__()
+        self.d = (self.zh * X_WAYS + self.x) * CORES + self.c
+        self.y, self.zl = self.expert % Y_WAYS, self.expert // Y_WAYS
+
+    def dp(self, far, core):
+        return ((self.zh + far[1]) % Z_WAYS * X_WAYS + (self.x + far[0]) % X_WAYS) * CORES + core
+
+    def other(self, far):
+        return (self.zl + far[1]) % PAIR * Y_WAYS + (self.y + far[0]) % Y_WAYS
+
+    def greet(self):
+        barrier = pltpu.get_barrier_semaphore()
+        peers = [(self.other(far), self.d) for far in FAR_EXPERT]
+        peers += [(self.expert, self.dp(far, core)) for far in FAR_DP for core in range(CORES)]
+        peers.append(self.partner())
+        for peer in peers:
+            pl.semaphore_signal(barrier, inc=1, device_id=peer, device_id_type=MESH)
+        pl.semaphore_wait(barrier, len(peers))
+
+
+def remote(src, dst, send_sem, recv_sem, peer):
+    return pltpu.make_async_remote_copy(
+        src_ref=src, dst_ref=dst, send_sem=send_sem, recv_sem=recv_sem,
+        device_id=peer, device_id_type=MESH,
+    )
+
+
+def dispatch_kernel(
+    pick_ref, x_ref, g_ref, out_ref, tok, away, mid, send1, recv1, send2, recv2
+):
+    me = Wide()
+    shard = x_ref.shape[1] // CORES
+    for h in range(CORES):
+        cols = slice(h * shard, (h + 1) * shard)
+        tok[h] = jnp.concatenate([x_ref[:, cols], g_ref[:, cols]], axis=1)
+    me.greet()
+
+    def picked(e, h):
+        return jnp.dot(pick_ref[e], tok[h], preferred_element_type=jnp.float32).astype(jnp.bfloat16)
+
+    def to_expert(h, k):
+        e = me.other(FAR_EXPERT[k])
+        return remote(
+            away.at[h, e], mid.at[h, me.expert], send1.at[h, k], recv1.at[h, me.expert], (e, me.d)
+        )
+
+    def to_shard(h, k, d):
+        return remote(
+            mid.at[h, d // CORES], out_ref.at[me.d // CORES, me.c], send2.at[h, k], recv2.at[me.d],
+            (me.expert, d),
+        )
+
+    for h in range(CORES):
+        for k, far in enumerate(FAR_EXPERT):
+            e = me.other(far)
+            away[h, e] = picked(e, h)
+            to_expert(h, k).start()
+        mid[h, me.expert] = picked(me.expert, h)
+
+    for h in range(CORES):
+        for k, far in enumerate(FAR_DP + ((0, 0),)):
+            d = me.dp(far, h)
+            src = d // CORES
+
+            @pl.when(src != me.expert)
+            def _():
+                remote(
+                    away.at[h, src], mid.at[h, src], send1.at[h, 0], recv1.at[h, src], (src, me.d)
+                ).wait_recv()
+
+            if far != (0, 0):
+                to_shard(h, k, d).start()
+            else:
+
+                @pl.when(me.c != h)
+                def _():
+                    to_shard(h, k, d).start()
+
+                @pl.when(me.c == h)
+                def _():
+                    out_ref[me.d // CORES, me.c] = mid[h, src]
+
+    def from_source(d):
+        return remote(mid.at[0, 0], out_ref.at[d // CORES, d % CORES], send2.at[0, 0], recv2.at[d], (me.expert, d))
+
+    for far in FAR_DP:
+        for core in range(CORES):
+            from_source(me.dp(far, core)).wait_recv()
+    from_source(me.dp((0, 0), 1 - me.c)).wait_recv()
+    for h in range(CORES):
+        for k, far in enumerate(FAR_EXPERT):
+            to_expert(h, k).wait_send()
+        for k, far in enumerate(FAR_DP):
+            to_shard(h, k, me.dp(far, h)).wait_send()
+
+        @pl.when(me.c != h)
+        def _():
+            to_shard(h, len(FAR_DP), me.dp((0, 0), h)).wait_send()
+
+
+def return_kernel(
+    low_ref, high_ref, dx_ref, out_ref, mid, back, send1, recv1, send2, recv2
+):
+    me = Wide()
+    me.greet()
+    shard = out_ref.shape[1] // CORES
+    near = me.dp((0, 0), 1 - me.c)
+
+    def to_block(k, d):
+        return remote(
+            dx_ref.at[d // CORES, d % CORES], mid.at[me.d // CORES, me.c], send1.at[k], recv1.at[me.d],
+            (me.expert, d),
+        )
+
+    def to_features(k):
+        e = me.other(FAR_EXPERT[k])
+        return remote(mid.at[e], back.at[me.expert], send2.at[k], recv2.at[me.expert], (e, me.d))
+
+    targets = [me.dp(far, core) for far in FAR_DP for core in range(CORES)] + [near]
+    for k, d in enumerate(targets):
+        to_block(k, d).start()
+    mid[me.d // CORES, me.c] = dx_ref[me.d // CORES, me.c]
+
+    def arrived(e):
+        for core in range(CORES):
+            d = e * CORES + core
+
+            @pl.when(d != me.d)
+            def _():
+                remote(
+                    dx_ref.at[0, 0], mid.at[e, core], send1.at[0], recv1.at[d], (me.expert, d)
+                ).wait_recv()
+
+    for k, far in enumerate(FAR_EXPERT):
+        arrived(me.other(far))
+        to_features(k).start()
+    arrived(me.expert)
+    back[me.expert] = mid[me.expert]
+    for far in FAR_EXPERT:
+        e = me.other(far)
+        remote(mid.at[0], back.at[e], send2.at[0], recv2.at[e], (e, me.d)).wait_recv()
+    parts = []
+    for h in range(CORES):
+        rows = back[:, h].reshape(low_ref.shape[1], CORES * shard)
+        low = jnp.dot(low_ref[...], rows, preferred_element_type=jnp.float32)
+        high = jnp.dot(high_ref[...], rows, preferred_element_type=jnp.float32)
+        parts.append(low[:, :shard] + high[:, shard:])
+    out_ref[...] = jnp.concatenate(parts, axis=1).astype(jnp.bfloat16)
+    for k, d in enumerate(targets):
+        to_block(k, d).wait_send()
+    for k in range(len(FAR_EXPERT)):
+        to_features(k).wait_send()
+
+
+def dispatched(pick, x, g):
+    (experts, rows, _), (tokens, width) = pick.shape, x.shape
+    bf16 = jnp.bfloat16
+    groups = X_WAYS * Z_WAYS
+    dma = pltpu.SemaphoreType.DMA
+    return pl.pallas_call(
+        dispatch_kernel,
+        out_shape=jax.ShapeDtypeStruct((groups, CORES, rows, width), bf16),
+        in_specs=vmem(3),
+        out_specs=vmem(1)[0],
+        scratch_shapes=[
+            pltpu.VMEM((CORES, tokens, width), bf16),
+            pltpu.VMEM((CORES, experts, rows, width), bf16),
+            pltpu.VMEM((CORES, experts, rows, width), bf16),
+            dma((CORES, len(FAR_EXPERT))),
+            dma((CORES, experts)),
+            dma((CORES, len(FAR_DP) + 1)),
+            dma((groups * CORES,)),
+        ],
+        compiler_params=pltpu.CompilerParams(
+            collective_id=2, has_side_effects=True, vmem_limit_bytes=20 << 20
+        ),
+    )(pick, x, g)
+
+
+def returned_rows(low, high, dx):
+    groups, cores, rows, width = dx.shape
+    tokens, bf16 = low.shape[0], jnp.bfloat16
+    experts = Y_WAYS * PAIR
+    dma = pltpu.SemaphoreType.DMA
+    return pl.pallas_call(
+        return_kernel,
+        out_shape=jax.ShapeDtypeStruct((tokens, width), bf16),
+        in_specs=vmem(3),
+        out_specs=vmem(1)[0],
+        scratch_shapes=[
+            pltpu.VMEM((experts, cores, rows, width), bf16),
+            pltpu.VMEM((experts, cores, rows, width), bf16),
+            dma((groups * cores,)),
+            dma((groups * cores,)),
+            dma((len(FAR_EXPERT),)),
+            dma((experts,)),
+        ],
+        compiler_params=pltpu.CompilerParams(
+            collective_id=3, has_side_effects=True, vmem_limit_bytes=20 << 20
+        ),
+    )(low, high, dx)
 
 
 def body(tokens, grad_out, expert_ids, route_weights, w_gate, w_up, w_down):
     experts = lax.axis_size("expert")
     groups = lax.axis_size("dp")
-    tok_rows, width = tokens.shape
+    tok_rows = tokens.shape[0]
     capacity = tok_rows // 2
     expert_index = lax.axis_index("expert")
     inv_root = 1.0 / math.sqrt(tok_rows * groups)
-    rows_first = (((0,), (0,)), ((), ()))
-    gate_shard, up_shard, down_shard = w_gate[0], w_up[0], w_down[0]
-    shard = gate_shard.shape[0]
-    halves = width // shard
+    gate_shard, up_shard, down_shard = w_gate[0], w_up[0], w_down[0].T
 
     names = jnp.arange(experts, dtype=jnp.int32)[:, None]
     hit0 = expert_ids[:, 0][None, :] == names
@@ -331,7 +533,12 @@
     rank = jnp.dot(hit, before, preferred_element_type=jnp.float32)
     rank = jnp.where(hit > 0, rank, -1.0).astype(jnp.int32)
     chosen = rank[:, None, :] == jnp.arange(capacity, dtype=jnp.int32)[None, :, None]
-    dispatch = chosen.astype(jnp.bfloat16).reshape(experts * capacity, tok_rows)
+    pick = chosen.astype(jnp.bfloat16)
+
+    def place(first):
+        part = rank.T[:, :, None] == jnp.arange(first, first + capacity // 2, dtype=jnp.int32)
+        return part.astype(jnp.bfloat16).reshape(tok_rows, experts * capacity // 2)
+
     weight_of = jnp.where(hit0, route_weights[:, 0][None, :], 0.0) + jnp.where(
         hit1, route_weights[:, 1][None, :], 0.0
     )
@@ -344,53 +551,11 @@
         axis=1,
     )
 
-    def send(rows):
-        picked = [
-            jnp.dot(
-                dispatch,
-                rows[:, h * shard : (h + 1) * shard],
-                preferred_element_type=jnp.float32,
-            )
-            .astype(jnp.bfloat16)
-            .reshape(experts, 1, capacity, shard)
-            for h in range(halves)
-        ]
-        moved = lax.all_to_all(
-            jnp.concatenate(picked, axis=1), "expert", split_axis=0, concat_axis=0, tiled=True
-        )
-        return lax.all_to_all(
-            moved.reshape(groups, capacity, shard), "dp", split_axis=0, concat_axis=0, tiled=True
-        ).reshape(groups // CORES, CORES, capacity, shard)
-
-    x_block = send(tokens)
-    g_block = send(grad_out)
-    act = summed_rows(x_block, g_block, gate_shard, up_shard, down_shard, own_weight[:, None])
-    grad_g, grad_u, grad_d, dx_rows = spread_rows(
-        inv_root, act, x_block, g_block, gate_shard, up_shard
-    )
-    returned = lax.all_to_all(
-        dx_rows.reshape(groups, capacity, shard), "dp", split_axis=0, concat_axis=0, tiled=True
-    )
-    returned = lax.all_to_all(
-        returned.reshape(experts, halves, capacity, shard),
-        "expert",
-        split_axis=0,
-        concat_axis=0,
-        tiled=True,
-    )
-    grad_tokens = jnp.concatenate(
-        [
-            lax.dot_general(
-                dispatch,
-                returned[:, h].reshape(experts * capacity, shard),
-                rows_first,
-                preferred_element_type=jnp.float32,
-            ).astype(jnp.bfloat16)
-            for h in range(halves)
-        ],
-        axis=1,
-    )
-    return (grad_tokens, grad_g[None], grad_u[None], grad_d[None])
+    packed = dispatched(pick, tokens, grad_out)
+    act = summed_rows(packed, gate_shard, up_shard, down_shard, own_weight[:, None])
+    grad_g, grad_u, grad_d, dx_rows = spread_rows(inv_root, act, packed, gate_shard, up_shard)
+    grad_tokens = returned_rows(place(0), place(capacity // 2), dx_rows)
+    return (grad_tokens, grad_g[None], grad_u[None], grad_d.T[None])
 
 
 def solution(mesh):

time: 272 us -> 227 us (0.83)
  Pallas kernels: 131 us -> 216 us
  blocking collectives: 65.6 us -> 0 us
  waiting for transfers between devices: 41.2 us -> 0 us
  starting transfers between devices: 14.5 us -> 0 us
  matrix products: 4.06 us -> 0.14 us
  local copies, waits for them, and re-layouts: 13.4 us -> 10 us
    pallas_call x0 -> x2, Pallas kernels: none -> 82.6 us  [the longest x1 50.7 us: dispatched(): pl.pallas_call(dispatch_kernel, out_shape=jax.ShapeDtypeStruct((groups, C...]
    all_to_all x3 -> x0, blocking collectives: 65.6 us -> none  [the longest x1 26.1 us: send(): lax.all_to_all(moved.reshape(groups, capacity, shard), 'dp', split_axis=0...]
    all_to_all x3 -> x0, waiting for transfers between devices: 41.2 us -> none  [the longest x1 14.4 us: send(): lax.all_to_all(jnp.concatenate(picked, axis=1), 'expert', split_axis=0, c...]
    all_to_all x3 -> x0, starting transfers between devices: 14.5 us -> none  [the longest x1 6.38 us: send(): lax.all_to_all(jnp.concatenate(picked, axis=1), 'expert', split_axis=0, c...]
    dot_general x6 -> x0, matrix products: 3.92 us -> none  [the longest x4 3.24 us: send(): jnp.dot(dispatch, rows[:, h * shard:(h + 1) * shard], preferred_element_t...]
    unnamed x15 -> x14, local copies, waits for them, and re-layouts: 10.4 us -> 8.12 us
  transfers between devices with their start and end apart: 3 -> 0, of which waited for: 3 -> 0; matrix products, arithmetic and copies ran while one was open for 3% -> 0% of each run, Pallas kernels for 0% -> 0%
where the time goes in v3:
time: 227 us
  Pallas kernels  216 us (95%)
  local copies, waits for them, and re-layouts  10 us (4%)
    pallas_call x1, Pallas kernels, spread_rows(): pl.pallas_call(functools.partial(spread_kernel, inv_root), out_shape=(jax...  69.7 us
    pallas_call x1, Pallas kernels, summed_rows(): pl.pallas_call(sum_kernel, out_shape=jax.ShapeDtypeStruct((CHUNKS, rows,...  63.5 us
    pallas_call x1, Pallas kernels, dispatched(): pl.pallas_call(dispatch_kernel, out_shape=jax.ShapeDtypeStruct((groups, C...  50.7 us
    pallas_call x1, Pallas kernels, returned_rows(): pl.pallas_call(return_kernel, out_shape=jax.ShapeDtypeStruct((tokens, wid...  31.9 us
    unnamed x14, local copies, waits for them, and re-layouts  8.12 us

profile of v3, /device:TPU:1, one launch (start us, length us, event | category | flops | bytes accessed | tf_op | source)
XLA Modules:
  0.0 227.0 jit_solution(14581764943093547970)
XLA Ops:
  0.6 0.8 slice_bitcast_fusion.3
  1.4 0.1 fusion.2
  1.5 0.8 slice_bitcast_fusion.1
  2.3 0.1 select_reduce_fusion
  2.4 0.1 copy.18.pw_ref
  2.6 0.0 copy-start.1
  2.6 0.9 copy-done.1
  3.5 0.0 copy-start.2
  3.5 0.9 copy-done.2
  4.5 50.7 %shard_map.102.rows_ref = bf16[8,2,64,896]{3,2,1,0:T(8,128)(2,1)S(1)} custom-call(bf16[8,64,128]{2,1,0:T(8,128)(2,1)S(1)} %fusion.pick_ref, bf16[128,896]{1,0:T(8,128)(2,1)S(1)} %copy-done.1, bf16[128,896]{1,0:T(8,128)(2,1)S(1)} %copy-done.2), custom_call_target="tpu_custom_call" | custom-call | tf_op jit(solution)/shard_map/pallas_call | solution.py:474
  55.1 0.0 copy-start
  55.1 63.5 %shard_map.103.act_ref = bf16[8,64,768]{2,1,0:T(8,128)(2,1)S(1)} custom-call(bf16[8,2,64,896]{3,2,1,0:T(8,128)(2,1)S(1)} %shard_map.102.rows_ref, bf16[448,2048]{1,0:T(8,128)(2,1)} %bitcast.29, bf16[448,2048]{1,0:T(8,128)(2,1)} %bitcast.31, bf16[448,2048]{1,0:T(8,128)(2,1)} %bitcast.35, f32[64,1]{1,0:T(8,128)S(1)} %copy.18.pw_ref), custom_call_target="tpu_custom_call" | custom-call | tf_op jit(solution)/shard_map/pallas_call | solution.py:257
  118.7 0.0 copy-done
  118.7 69.7 %shard_map.104 = (bf16[448,2048]{1,0:T(8,128)(2,1)S(1)}, bf16[448,2048]{1,0:T(8,128)(2,1)}, bf16[448,2048]{1,0:T(8,128)(2,1)}, bf16[8,2,32,896]{3,2,1,0:T(8,128)(2,1)S(1)}) custom-call(bf16[8,64,768]{2,1,0:T(8,128)(2,1)S(1)} %shard_map.103.act_ref, bf16[8,2,64,896]{3,2,1,0:T(8,128)(2,1)} %copy-done, bf16[448,2048]{1,0:T(8,128)(2,1)} %bitcast.30, ...), custom_call_target="tpu_custom_call" | custom-call | tf_op jit(solution)/shard_map/pallas_call | solution.py:284
  188.5 0.1 copy.16
  188.6 0.1 eq.129
  188.7 0.1 eq.125
  188.8 31.9 %shard_map.105 = bf16[128,896]{1,0:T(8,128)(2,1)S(1)} custom-call(bf16[128,256]{1,0:T(8,128)(2,1)S(1)} %get-tuple-element.13.low_ref, bf16[128,256]{1,0:T(8,128)(2,1)S(1)} %get-tuple-element.12.high_ref, bf16[8,2,32,896]{3,2,1,0:T(8,128)(2,1)S(1)} %get-tuple-element.8.dx_ref), custom_call_target="tpu_custom_call" | custom-call | tf_op jit(solution)/shard_map/pallas_call | solution.py:499
  220.8 0.7 copy.23
  221.4 1.2 copy.24
  222.7 0.9 copy-done.4
  223.6 1.2 copy.25
  224.8 0.9 copy-done.3
  225.8 1.2 copy.26
  (11 shorter events, 0.1 us)
Async XLA Ops:
  2.6 0.9 copy-start.1
  3.5 0.9 copy-start.2
  55.1 63.6 %copy-start = (bf16[8,2,64,896]{3,2,1,0:T(8,128)(2,1)}, bf16[8,2,64,896]{3,2,1,0:T(8,128)(2,1)S(1)}, u32[]{:S(2)}) copy-start(bf16[8,2,64,896]{3,2,1,0:T(8,128)(2,1)S(1)} %shard_map.102.rows_ref) | copy-start | bytes 5505028
  221.4 2.2 copy-start.4
  223.6 2.2 copy-start.3

commit v4 on v3

v4 whole, which is shorter than its diff:
```python
import functools
import math

import jax
import jax.numpy as jnp
from jax import lax
from jax.experimental import pallas as pl
from jax.experimental.pallas import tpu as pltpu
from jax.sharding import PartitionSpec as P

MESH = pl.DeviceIdType.MESH
CHUNKS = 8
X_WAYS, Z_WAYS, CORES = 4, 2, 2
LAST = (((1,), (1,)), ((), ()))
SUM_ORDER = "zxzxzxzx"
SPREAD_ORDER = "xzxzxzxzxzxz"
SUM_LAGS = (0, 1, 3, 4, 6)
SPREAD_LAGS = (0, 1, 3, 4)


class Place:
    def __init__(self):
        self.expert = lax.axis_index("expert")
        d = lax.axis_index("dp")
        self.c = d % CORES
        self.x = (d // CORES) % X_WAYS
        self.zh = d // (CORES * X_WAYS)

    def at(self, zh, x, c):
        return (self.expert, (zh * X_WAYS + x) * CORES + c)

    def partner(self):
        return self.at(self.zh, self.x, 1 - self.c)

    def opposite(self):
        return self.at(1 - self.zh, self.x, self.c)

    def along_x(self, k):
        return (self.x + k) % X_WAYS

    def ring(self, k):
        return self.at(self.zh, self.along_x(k), self.c)

    def greet(self):
        barrier = pltpu.get_barrier_semaphore()
        peers = [self.partner(), self.opposite()] + [self.ring(k) for k in range(1, X_WAYS)]
        for peer in peers:
            pl.semaphore_signal(barrier, inc=1, device_id=peer, device_id_type=MESH)
        pl.semaphore_wait(barrier, len(peers))


def remote(src, dst, send_sem, recv_sem, peer):
    return pltpu.make_async_remote_copy(
        src_ref=src, dst_ref=dst, send_sem=send_sem, recv_sem=recv_sem,
        device_id=peer, device_id_type=MESH,
    )


def sum_kernel(
    rows_ref, wg_ref, wu_ref, wd_ref, pw_ref, out_ref,
    xp, gp, away, arrived, held, first, second, send_sem, recv_sem,
):
    me = Place()
    me.greet()
    n = wg_ref.shape[1] // CHUNKS
    blocks, rows, shard = X_WAYS * Z_WAYS, rows_ref.shape[2], wg_ref.shape[0]
    low, high = pl.ds(0, rows // 2), pl.ds(rows // 2, rows // 2)
    here, up, down, far = me.x, me.along_x(1), me.along_x(3), me.along_x(2)
    f32 = jnp.float32

    for i in range(blocks):
        at = pl.ds(i * rows, rows)
        for which in range(CORES):
            both = rows_ref[i, me.c if which == 0 else 1 - me.c]
            xp[which, at, :] = both[:, :shard]
            gp[which, at, :] = both[:, shard:]

    def copy(j, lane, src, dst, peer):
        return remote(src, dst, send_sem.at[j, lane], recv_sem.at[j, lane], peer)

    def add(ref, more):
        ref[...] = (ref[...].astype(f32) + more.astype(f32)).astype(jnp.bfloat16)

    def products(j, which, dst):
        cols = pl.ds(j * n, n)
        parts = (
            jnp.dot(xp[which], wg_ref[:, cols], preferred_element_type=f32),
            jnp.dot(xp[which], wu_ref[:, cols], preferred_element_type=f32),
            jnp.dot(gp[which], wd_ref[:, cols], preferred_element_type=f32),
        )
        for k, part in enumerate(parts):
            dst[j, :, :, :, k * n : (k + 1) * n] = part.astype(jnp.bfloat16).reshape(
                Z_WAYS, X_WAYS, rows, n
            )

    def to_partner(j):
        return copy(j, 0, away.at[j], arrived.at[j], me.partner())

    def opposite(j):
        if SUM_ORDER[j] == "x":
            return copy(j, 1, held.at[j, 1 - me.zh, here], first.at[j, 4], me.opposite())
        return copy(j, 1, held.at[j, 1 - me.zh], first.at[j, pl.ds(0, X_WAYS)], me.opposite())

    def ring_first(j, lanes=(0, 1, 2, 3)):
        mine = held.at[j, me.zh]
        if SUM_ORDER[j] == "x":
            table = (
                (held.at[j, 0, far], first.at[j, 0]),
                (held.at[j, 1, far], first.at[j, 1]),
                (held.at[j, 1, up], first.at[j, 2]),
                (held.at[j, 0, down], first.at[j, 3]),
            )
        else:
            table = (
                (mine.at[far, low], second.at[j, 2, low]),
                (mine.at[far, high], second.at[j, 2, high]),
                (mine.at[up, high], second.at[j, 0, high]),
                (mine.at[down, low], second.at[j, 1, low]),
            )
        return [copy(j, 2 + i, *table[i], me.ring(1 + 2 * (i % 2))) for i in lanes]

    def ring_second(j):
        if SUM_ORDER[j] == "x":
            return [
                copy(j, 6, held.at[j, 0, up], second.at[j, 0], me.ring(1)),
                copy(j, 7, held.at[j, 1, down], second.at[j, 1], me.ring(3)),
            ]
        mine = held.at[j, me.zh]
        return [
            copy(j, 6, mine.at[up, low], second.at[j, 0, low], me.ring(1)),
            copy(j, 7, mine.at[down, high], second.at[j, 1, high], me.ring(3)),
        ]

    def arrive(copies):
        for one in copies:
            one.wait_recv()

    def start(copies):
        for one in copies:
            one.start()

    def make(j):
        products(j, 1, away)
        to_partner(j).start()
        products(j, 0, held)

    def cores(j):
        arrive([to_partner(j)])
        for z in range(Z_WAYS):
            add(held.at[j, z], arrived[j, z])
        start(ring_first(j) if SUM_ORDER[j] == "x" else [opposite(j)])

    def pass_on(j):
        copies = ring_second(j)
        if SUM_ORDER[j] == "x":
            arrive(ring_first(j, (0,)))
            add(held.at[j, 0, up], first[j, 0])
            copies[0].start()
            arrive(ring_first(j, (1,)))
            add(held.at[j, 1, down], first[j, 1])
            copies[1].start()
        else:
            arrive(ring_first(j, (0,)))
            add(held.at[j, me.zh, up, low], second[j, 2, low])
            copies[0].start()
            arrive(ring_first(j, (1,)))
            add(held.at[j, me.zh, down, high], second[j, 2, high])
            copies[1].start()

    def gather(j):
        if SUM_ORDER[j] == "x":
            arrive(ring_first(j, (2, 3)) + ring_second(j))
            for z, (one, two) in enumerate(((second.at[j, 0], first.at[j, 3]), (second.at[j, 1], first.at[j, 2]))):
                add(held.at[j, z, here], one[...].astype(f32) + two[...].astype(f32))
            start([opposite(j)])
        else:
            arrive([opposite(j)])
            for x in (me.along_x(2), me.along_x(1), me.along_x(3), me.x):
                add(held.at[j, me.zh, x], first[j, x])
            start(ring_first(j))

    def finish(j):
        total = held[j, me.zh, here].astype(f32)
        if SUM_ORDER[j] == "x":
            arrive([opposite(j)])
            total += first[j, 4].astype(f32)
        else:
            arrive(ring_first(j, (2, 3)) + ring_second(j))
            total += second[j, 0].astype(f32) + second[j, 1].astype(f32)
        weight = pw_ref[...]
        gate, upper, back = total[:, :n], total[:, n : 2 * n], total[:, 2 * n :] * weight
        s = 1.0 / (1.0 + jnp.exp(-gate))
        out_ref[j, :, :n] = (back * upper * s * (1.0 + gate * (1.0 - s))).astype(jnp.bfloat16)
        out_ref[j, :, n:] = (back * gate * s).astype(jnp.bfloat16)
        at = (j % 2) * n
        out_ref[CHUNKS + j // 2, :, at : at + n] = (weight * gate * s * upper).astype(jnp.bfloat16)

    def middle(j, step):
        order = (pass_on, gather) if SUM_ORDER[j] == "x" else (gather, pass_on)
        order[step](j)

    stages = (make, cores, lambda j: middle(j, 0), lambda j: middle(j, 1), finish)
    for t in range(CHUNKS + SUM_LAGS[-1]):
        for stage, lag in zip(stages, SUM_LAGS):
            if 0 <= t - lag < CHUNKS:
                stage(t - lag)
    for j in range(CHUNKS):
        for one in [to_partner(j), opposite(j)] + ring_first(j) + ring_second(j):
            one.wait_send()


def vmem(count):
    return [pl.BlockSpec(memory_space=pltpu.VMEM)] * count


def summed_rows(packed, w_gate, w_up, w_down, weight):
    (blocks, cores, rows, _), (shard, hidden) = packed.shape, w_gate.shape
    cols = 3 * hidden // CHUNKS
    bf16 = jnp.bfloat16
    return pl.pallas_call(
        sum_kernel,
        out_shape=jax.ShapeDtypeStruct((CHUNKS * 3 // 2, rows, 2 * hidden // CHUNKS), bf16),
        in_specs=vmem(5),
        out_specs=vmem(1)[0],
        scratch_shapes=[
            pltpu.VMEM((cores, blocks * rows, shard), bf16),
            pltpu.VMEM((cores, blocks * rows, shard), bf16),
            pltpu.VMEM((CHUNKS, Z_WAYS, X_WAYS, rows, cols), bf16),
            pltpu.VMEM((CHUNKS, Z_WAYS, X_WAYS, rows, cols), bf16),
            pltpu.VMEM((CHUNKS, Z_WAYS, X_WAYS, rows, cols), bf16),
            pltpu.VMEM((CHUNKS, X_WAYS + 1, rows, cols), bf16),
            pltpu.VMEM((CHUNKS, X_WAYS - 1, rows, cols), bf16),
            pltpu.SemaphoreType.DMA((CHUNKS, 8)),
            pltpu.SemaphoreType.DMA((CHUNKS, 8)),
        ],
        compiler_params=pltpu.CompilerParams(
            collective_id=0, has_side_effects=True, vmem_limit_bytes=50 << 20
        ),
    )(packed, w_gate, w_up, w_down, weight)


FAR_DP = ((2, 1), (1, 1), (3, 1), (2, 0), (0, 1), (1, 0), (3, 0))
FAR_EXPERT = ((2, 1), (1, 1), (3, 1), (2, 0), (1, 0), (3, 0), (0, 1))
Y_WAYS, PAIR = 4, 2


class Wide(Place):
    def __init__(self):
        super().__init__()
        self.d = (self.zh * X_WAYS + self.x) * CORES + self.c
        self.y, self.zl = self.expert % Y_WAYS, self.expert // Y_WAYS

    def dp(self, far, core):
        return ((self.zh + far[1]) % Z_WAYS * X_WAYS + (self.x + far[0]) % X_WAYS) * CORES + core

    def other(self, far):
        return (self.zl + far[1]) % PAIR * Y_WAYS + (self.y + far[0]) % Y_WAYS

    def greet(self):
        barrier = pltpu.get_barrier_semaphore()
        peers = [(self.other(far), self.d) for far in FAR_EXPERT]
        peers += [(self.expert, self.dp(far, core)) for far in FAR_DP for core in range(CORES)]
        peers.append(self.partner())
        for peer in peers:
            pl.semaphore_signal(barrier, inc=1, device_id=peer, device_id_type=MESH)
        pl.semaphore_wait(barrier, len(peers))


def dispatch_kernel(
    pick_ref, x_ref, g_ref, out_ref, tok, away, mid, send1, recv1, send2, recv2
):
    me = Wide()
    shard = x_ref.shape[1] // CORES
    for h in range(CORES):
        cols = slice(h * shard, (h + 1) * shard)
        tok[h] = jnp.concatenate([x_ref[:, cols], g_ref[:, cols]], axis=1)
    me.greet()

    def picked(e, h):
        return jnp.dot(pick_ref[e], tok[h], preferred_element_type=jnp.float32).astype(jnp.bfloat16)

    def to_expert(h, k):
        e = me.other(FAR_EXPERT[k])
        return remote(
            away.at[h, e], mid.at[h, me.expert], send1.at[h, k], recv1.at[h, me.expert], (e, me.d)
        )

    def to_shard(h, k, d):
        return remote(
            mid.at[h, d // CORES], out_ref.at[me.d // CORES, me.c], send2.at[h, k], recv2.at[me.d],
            (me.expert, d),
        )

    for h in range(CORES):
        for k, far in enumerate(FAR_EXPERT):
            e = me.other(far)
            away[h, e] = picked(e, h)
            to_expert(h, k).start()
        mid[h, me.expert] = picked(me.expert, h)

    for h in range(CORES):
        for k, far in enumerate(FAR_DP + ((0, 0),)):
            d = me.dp(far, h)
            src = d // CORES

            @pl.when(src != me.expert)
            def _():
                remote(
                    away.at[h, src], mid.at[h, src], send1.at[h, 0], recv1.at[h, src], (src, me.d)
                ).wait_recv()

            if far != (0, 0):
                to_shard(h, k, d).start()
            else:

                @pl.when(me.c != h)
                def _():
                    to_shard(h, k, d).start()

                @pl.when(me.c == h)
                def _():
                    out_ref[me.d // CORES, me.c] = mid[h, src]

    def from_source(d):
        return remote(mid.at[0, 0], out_ref.at[d // CORES, d % CORES], send2.at[0, 0], recv2.at[d], (me.expert, d))

    for far in FAR_DP:
        for core in range(CORES):
            from_source(me.dp(far, core)).wait_recv()
    from_source(me.dp((0, 0), 1 - me.c)).wait_recv()
    for h in range(CORES):
        for k, far in enumerate(FAR_EXPERT):
            to_expert(h, k).wait_send()
        for k, far in enumerate(FAR_DP):
            to_shard(h, k, me.dp(far, h)).wait_send()

        @pl.when(me.c != h)
        def _():
            to_shard(h, len(FAR_DP), me.dp((0, 0), h)).wait_send()


def spread_kernel(
    inv_root, act_ref, rows_ref, wg_ref, wu_ref, low_ref, high_ref, gg_ref, gu_ref, gd_ref, out_ref,
    xt, gt, whole, total, dx, mid, back, send_sem, recv_sem, send1, recv1, send2, recv2,
):
    me = Wide()
    me.greet()
    n = wg_ref.shape[1] // CHUNKS
    blocks, rows, shard = X_WAYS * Z_WAYS, rows_ref.shape[2], wg_ref.shape[0]
    slots = CORES * blocks * rows
    low, high = pl.ds(0, rows // 2), pl.ds(rows // 2, rows // 2)
    here, up, down = me.x, me.along_x(1), me.along_x(3)
    f32 = jnp.float32
    spread_chunks = len(SPREAD_ORDER)

    def copy(j, lane, src, dst, peer):
        return remote(src, dst, send_sem.at[j, lane], recv_sem.at[j, lane], peer)

    def part(j, x, half=None):
        if half is None:
            return whole.at[j, 0, me.zh, x] if SPREAD_ORDER[j] == "x" else whole.at[j, 0, :, x]
        return whole.at[j, 0, me.zh, x, half] if SPREAD_ORDER[j] == "x" else whole.at[j, 0, :, x, half]

    def neighbours(j):
        src = act_ref.at[j] if SPREAD_ORDER[j] == "x" else part(j, here)
        return [copy(j, 2, src, part(j, here), me.ring(1)), copy(j, 3, src, part(j, here), me.ring(3))]

    def passed(j):
        return [
            copy(j, 4, part(j, down, low), part(j, down, low), me.ring(1)),
            copy(j, 5, part(j, up, high), part(j, up, high), me.ring(3)),
        ]

    def opposite(j):
        if SPREAD_ORDER[j] == "x":
            return copy(j, 1, whole.at[j, 0, me.zh], whole.at[j, 0, me.zh], me.opposite())
        return copy(j, 1, act_ref.at[j], whole.at[j, 0, me.zh, here], me.opposite())

    def to_partner(j):
        return copy(j, 0, whole.at[j, 0], whole.at[j, 1], me.partner())

    def begin(j):
        if SPREAD_ORDER[j] == "x":
            for one in neighbours(j):
                one.start()
        else:
            opposite(j).start()
        whole[j, 0, me.zh, here] = act_ref[j]

    def relay(j):
        for one, on in zip(neighbours(j), passed(j)):
            one.wait_recv()
            on.start()

    def middle(j, step):
        if SPREAD_ORDER[j] == "x":
            if step == 0:
                relay(j)
            else:
                for one in passed(j):
                    one.wait_recv()
                opposite(j).start()
        elif step == 0:
            opposite(j).wait_recv()
            for one in neighbours(j):
                one.start()
        else:
            relay(j)

    def cores(j):
        if SPREAD_ORDER[j] == "x":
            opposite(j).wait_recv()
        else:
            for one in passed(j):
                one.wait_recv()
        to_partner(j).start()

    def grad(turned, j, cols):
        both = whole[j, :, :, :, :, cols].reshape(slots, -1)
        return (jnp.dot(turned[...], both, preferred_element_type=f32) * inv_root).astype(jnp.bfloat16)

    def inputs(j):
        to_partner(j).wait_recv()
        cols = pl.ds(j * n, n)
        d_gate = whole[j, :, :, :, :, :n].reshape(slots, n)
        d_up = whole[j, :, :, :, :, n:].reshape(slots, n)
        more = lax.dot_general(d_gate, wg_ref[:, cols], LAST, preferred_element_type=f32)
        more += lax.dot_general(d_up, wu_ref[:, cols], LAST, preferred_element_type=f32)
        total[...] = more if j == 0 else total[...] + more

    def weights(j):
        if j < CHUNKS:
            cols = pl.ds(j * n, n)
            gg_ref[:, cols] = grad(xt, j, slice(0, n))
            gu_ref[:, cols] = grad(xt, j, slice(n, 2 * n))
        else:
            to_partner(j).wait_recv()
            gd_ref[:, pl.ds((j - CHUNKS) * 2 * n, 2 * n)] = grad(gt, j, slice(0, 2 * n))

    near = me.dp((0, 0), 1 - me.c)
    targets = [me.dp(far, core) for far in FAR_DP for core in range(CORES)] + [near]

    def to_block(k, d):
        return remote(
            dx.at[d // CORES, d % CORES], mid.at[me.d // CORES, me.c], send1.at[k], recv1.at[me.d],
            (me.expert, d),
        )

    def to_features(k):
        e = me.other(FAR_EXPERT[k])
        return remote(mid.at[e], back.at[me.expert], send2.at[k], recv2.at[me.expert], (e, me.d))

    def home_first():
        for i in range(blocks):
            for which in range(CORES):
                at = (which * blocks + i) * rows
                one = total[at : at + rows // 2, :].astype(jnp.bfloat16)
                two = total[at + rows // 2 : at + rows, :].astype(jnp.bfloat16)
                dx[i, me.c if which == 0 else 1 - me.c] = jnp.concatenate([one, two], axis=1)
        for k, d in enumerate(targets):
            to_block(k, d).start()
        mid[me.d // CORES, me.c] = dx[me.d // CORES, me.c]

    def arrived(e):
        for core in range(CORES):
            d = e * CORES + core

            @pl.when(d != me.d)
            def _():
                remote(
                    dx.at[0, 0], mid.at[e, core], send1.at[0], recv1.at[d], (me.expert, d)
                ).wait_recv()

    def home_second():
        for k, far in enumerate(FAR_EXPERT):
            arrived(me.other(far))
            to_features(k).start()
        arrived(me.expert)
        back[me.expert] = mid[me.expert]

    def home():
        for far in FAR_EXPERT:
            e = me.other(far)
            remote(mid.at[0], back.at[e], send2.at[0], recv2.at[e], (e, me.d)).wait_recv()
        parts = []
        for h in range(CORES):
            blocks_of = back[:, h].reshape(low_ref.shape[1], CORES * shard)
            one = jnp.dot(low_ref[...], blocks_of, preferred_element_type=f32)
            two = jnp.dot(high_ref[...], blocks_of, preferred_element_type=f32)
            parts.append(one[:, :shard] + two[:, shard:])
        out_ref[...] = jnp.concatenate(parts, axis=1).astype(jnp.bfloat16)

    for j in range(spread_chunks):
        begin(j)
    for lo, turned in ((0, xt), (shard, gt)):
        for i in range(blocks):
            for which in range(CORES):
                at = pl.ds((which * blocks + i) * rows, rows)
                c = me.c if which == 0 else 1 - me.c
                total[at, :] = rows_ref[i, c][:, lo : lo + shard].astype(f32)
        turned[...] = total[...].T.astype(jnp.bfloat16)

    def products(j):
        if j < CHUNKS:
            inputs(j)
        if j == CHUNKS - 1:
            home_first()
        if j < CHUNKS:
            weights(j)

    stages = (lambda j: middle(j, 0), lambda j: middle(j, 1), cores, products)
    for t in range(spread_chunks + SPREAD_LAGS[-1]):
        for stage, lag in zip(stages, SPREAD_LAGS):
            if 0 <= t - lag < spread_chunks:
                stage(t - lag)
    home_second()
    for j in range(CHUNKS, spread_chunks):
        weights(j)
    home()
    for j in range(spread_chunks):
        for one in [to_partner(j), opposite(j)] + neighbours(j) + passed(j):
            one.wait_send()
    for k, d in enumerate(targets):
        to_block(k, d).wait_send()
    for k in range(len(FAR_EXPERT)):
        to_features(k).wait_send()


def dispatched(pick, x, g):
    (experts, rows, _), (tokens, width) = pick.shape, x.shape
    bf16 = jnp.bfloat16
    groups = X_WAYS * Z_WAYS
    dma = pltpu.SemaphoreType.DMA
    return pl.pallas_call(
        dispatch_kernel,
        out_shape=jax.ShapeDtypeStruct((groups, CORES, rows, width), bf16),
        in_specs=vmem(3),
        out_specs=vmem(1)[0],
        scratch_shapes=[
            pltpu.VMEM((CORES, tokens, width), bf16),
            pltpu.VMEM((CORES, experts, rows, width), bf16),
            pltpu.VMEM((CORES, experts, rows, width), bf16),
            dma((CORES, len(FAR_EXPERT))),
            dma((CORES, experts)),
            dma((CORES, len(FAR_DP) + 1)),
            dma((groups * CORES,)),
        ],
        compiler_params=pltpu.CompilerParams(
            collective_id=2, has_side_effects=True, vmem_limit_bytes=20 << 20
        ),
    )(pick, x, g)


def spread_rows(inv_root, act, packed, w_gate, w_up, low, high):
    (blocks, cores, rows, width), (shard, hidden) = packed.shape, w_gate.shape
    cols = 2 * hidden // CHUNKS
    slots = cores * blocks * rows
    experts = Y_WAYS * PAIR
    count = len(SPREAD_ORDER)
    bf16, dma = jnp.bfloat16, pltpu.SemaphoreType.DMA
    return pl.pallas_call(
        functools.partial(spread_kernel, inv_root),
        out_shape=(
            jax.ShapeDtypeStruct((shard, hidden), bf16),
            jax.ShapeDtypeStruct((shard, hidden), bf16),
            jax.ShapeDtypeStruct((shard, hidden), bf16),
            jax.ShapeDtypeStruct((low.shape[0], width), bf16),
        ),
        in_specs=vmem(6),
        out_specs=vmem(4),
        scratch_shapes=[
            pltpu.VMEM((shard, slots), bf16),
            pltpu.VMEM((shard, slots), bf16),
            pltpu.VMEM((count, cores, Z_WAYS, X_WAYS, rows, cols), bf16),
            pltpu.VMEM((slots, shard), jnp.float32),
            pltpu.VMEM((blocks, cores, rows // 2, width), bf16),
            pltpu.VMEM((experts, cores, rows // 2, width), bf16),
            pltpu.VMEM((experts, cores, rows // 2, width), bf16),
            dma((count, 6)),
            dma((count, 6)),
            dma((blocks * cores,)),
            dma((blocks * cores,)),
            dma((len(FAR_EXPERT),)),
            dma((experts,)),
        ],
        compiler_params=pltpu.CompilerParams(
            collective_id=1, has_side_effects=True, vmem_limit_bytes=50 << 20
        ),
    )(act, packed, w_gate, w_up, low, high)


def body(tokens, grad_out, expert_ids, route_weights, w_gate, w_up, w_down):
    experts = lax.axis_size("expert")
    groups = lax.axis_size("dp")
    tok_rows = tokens.shape[0]
    capacity = tok_rows // 2
    expert_index = lax.axis_index("expert")
    inv_root = 1.0 / math.sqrt(tok_rows * groups)
    gate_shard, up_shard, down_shard = w_gate[0], w_up[0], w_down[0].T

    names = jnp.arange(experts, dtype=jnp.int32)[:, None]
    hit0 = expert_ids[:, 0][None, :] == names
    hit1 = expert_ids[:, 1][None, :] == names
    hit = (hit0 | hit1).astype(jnp.bfloat16)
    index = jnp.arange(tok_rows, dtype=jnp.int32)
    before = (index[:, None] < index[None, :]).astype(jnp.bfloat16)
    rank = jnp.dot(hit, before, preferred_element_type=jnp.float32)
    rank = jnp.where(hit > 0, rank, -1.0).astype(jnp.int32)
    chosen = rank[:, None, :] == jnp.arange(capacity, dtype=jnp.int32)[None, :, None]
    pick = chosen.astype(jnp.bfloat16)

    def place(first):
        part = rank.T[:, :, None] == jnp.arange(first, first + capacity // 2, dtype=jnp.int32)
        return part.astype(jnp.bfloat16).reshape(tok_rows, experts * capacity // 2)

    weight_of = jnp.where(hit0, route_weights[:, 0][None, :], 0.0) + jnp.where(
        hit1, route_weights[:, 1][None, :], 0.0
    )
    own_rank = lax.dynamic_slice_in_dim(rank, expert_index, 1)
    own_weight_of = lax.dynamic_slice_in_dim(weight_of, expert_index, 1)
    own_weight = jnp.sum(
        jnp.where(
            own_rank == jnp.arange(capacity, dtype=jnp.int32)[:, None], own_weight_of, 0.0
        ),
        axis=1,
    )

    packed = dispatched(pick, tokens, grad_out)
    act = summed_rows(packed, gate_shard, up_shard, down_shard, own_weight[:, None])
    grad_g, grad_u, grad_d, grad_tokens = spread_rows(
        inv_root, act, packed, gate_shard, up_shard, place(0), place(capacity // 2)
    )
    return (grad_tokens, grad_g[None], grad_u[None], grad_d.T[None])


def solution(mesh):
    in_specs = (
        P("dp", "expert"),
        P("dp", "expert"),
        P("dp", None),
        P("dp", None),
        P("expert", "dp", None),
        P("expert", "dp", None),
        P("expert", None, "dp"),
    )
    out_specs = (
        P("dp", "expert"),
        P("expert", "dp", None),
        P("expert", "dp", None),
        P("expert", None, "dp"),
    )
    return jax.shard_map(body, mesh=mesh, in_specs=in_specs, out_specs=out_specs, check_vma=False)
```

time: 227 us -> 213 us (0.938)
  Pallas kernels: 216 us -> 202 us
    pallas_call x2 -> x1, Pallas kernels: 95.5 us -> 59.7 us  [summed_rows(): pl.pallas_call(sum_kernel, out_shape=jax.ShapeDtypeStruct((CHUNKS * 3 //...]
    pallas_call x1, Pallas kernels: 69.7 us -> 91.2 us  [spread_rows(): pl.pallas_call(functools.partial(spread_kernel, inv_root), out_shape=(jax...]
where the time goes in v4:
time: 213 us
  Pallas kernels  202 us (95%)
  local copies, waits for them, and re-layouts  10 us (5%)
    pallas_call x1, Pallas kernels, spread_rows(): pl.pallas_call(functools.partial(spread_kernel, inv_root), out_shape=(jax...  91.2 us
    pallas_call x1, Pallas kernels, summed_rows(): pl.pallas_call(sum_kernel, out_shape=jax.ShapeDtypeStruct((CHUNKS * 3 //...  59.7 us
    pallas_call x1, Pallas kernels, dispatched(): pl.pallas_call(dispatch_kernel, out_shape=jax.ShapeDtypeStruct((groups, C...  50.7 us
    unnamed x14, local copies, waits for them, and re-layouts  8.12 us

profile of v4, /device:TPU:1, one launch (start us, length us, event | category | flops | bytes accessed | tf_op | source)
XLA Modules:
  0.0 212.6 jit_solution(9585207044603465173)
XLA Ops:
  0.6 0.8 slice_bitcast_fusion.3
  1.4 0.8 slice_bitcast_fusion.1
  2.2 0.1 eq.136
  2.2 0.1 eq.132
  2.3 0.1 select_add_fusion
  2.5 0.1 select_reduce_fusion
  2.6 0.1 copy.16.pw_ref
  2.7 0.1 copy.17
  2.9 0.0 copy-start.1
  2.9 0.9 copy-done.1
  3.8 0.0 copy-start.2
  3.8 0.9 copy-done.2
  4.8 50.7 %shard_map.102.rows_ref = bf16[8,2,64,896]{3,2,1,0:T(8,128)(2,1)S(1)} custom-call(bf16[8,64,128]{2,1,0:T(8,128)(2,1)S(1)} %fusion.pick_ref, bf16[128,896]{1,0:T(8,128)(2,1)S(1)} %copy-done.1, bf16[128,896]{1,0:T(8,128)(2,1)S(1)} %copy-done.2), custom_call_target="tpu_custom_call" | custom-call | tf_op jit(solution)/shard_map/pallas_call | solution.py:534
  55.4 0.0 copy-start
  55.5 59.7 %shard_map.103.act_ref = bf16[12,64,512]{2,1,0:T(8,128)(2,1)S(1)} custom-call(bf16[8,2,64,896]{3,2,1,0:T(8,128)(2,1)S(1)} %shard_map.102.rows_ref, bf16[448,2048]{1,0:T(8,128)(2,1)} %bitcast.29, bf16[448,2048]{1,0:T(8,128)(2,1)} %bitcast.31, bf16[448,2048]{1,0:T(8,128)(2,1)} %bitcast.35, f32[64,1]{1,0:T(8,128)S(1)} %copy.16.pw_ref), custom_call_target="tpu_custom_call" | custom-call | tf_op jit(solution)/shard_map/pallas_call | solution.py:220
  115.1 0.0 copy-done
  115.2 91.2 %shard_map.104 = (bf16[448,2048]{1,0:T(8,128)(2,1)S(1)}, bf16[448,2048]{1,0:T(8,128)(2,1)}, bf16[448,2048]{1,0:T(8,128)(2,1)}, bf16[128,896]{1,0:T(8,128)(2,1)S(1)}) custom-call(bf16[12,64,512]{2,1,0:T(8,128)(2,1)S(1)} %shard_map.103.act_ref, bf16[8,2,64,896]{3,2,1,0:T(8,128)(2,1)} %copy-done, bf16[448,2048]{1,0:T(8,128)(2,1)} %bitcast.30, ...), custom_call_target="tpu_custom_call" | custom-call | tf_op jit(solution)/shard_map/pallas_call | solution.py:561
  206.4 0.7 copy.23
  207.1 0.0 copy-start.4
  207.1 1.2 copy.24
  208.3 0.9 copy-done.4
  209.2 1.2 copy.25
  210.4 0.9 copy-done.3
  211.4 1.2 copy.26
  (10 shorter events, 0.1 us)
Async XLA Ops:
  2.9 0.9 copy-start.1
  3.8 0.9 copy-start.2
  55.4 59.7 %copy-start = (bf16[8,2,64,896]{3,2,1,0:T(8,128)(2,1)}, bf16[8,2,64,896]{3,2,1,0:T(8,128)(2,1)S(1)}, u32[]{:S(2)}) copy-start(bf16[8,2,64,896]{3,2,1,0:T(8,128)(2,1)S(1)} %shard_map.102.rows_ref) | copy-start | bytes 5505028
  207.1 2.2 %copy-start.4 = (bf16[448,2048]{1,0:T(8,128)(2,1)S(1)}, bf16[448,2048]{1,0:T(8,128)(2,1)}, u32[]{:S(2)}) copy-start(bf16[448,2048]{1,0:T(8,128)(2,1)} %get-tuple-element.10) | copy-start | bytes 5505028
  209.2 2.2 %copy-start.3 = (bf16[448,2048]{1,0:T(8,128)(2,1)S(1)}, bf16[448,2048]{1,0:T(8,128)(2,1)}, u32[]{:S(2)}) copy-start(bf16[448,2048]{1,0:T(8,128)(2,1)} %get-tuple-element.11) | copy-start | bytes 5505028

commit v5 on v4

--- a/solution.py
+++ b/solution.py
@@ -12,10 +12,11 @@
 CHUNKS = 8
 X_WAYS, Z_WAYS, CORES = 4, 2, 2
 LAST = (((1,), (1,)), ((), ()))
-SUM_ORDER = "zxzxzxzx"
-SPREAD_ORDER = "xzxzxzxzxzxz"
-SUM_LAGS = (0, 1, 3, 4, 6)
-SPREAD_LAGS = (0, 1, 3, 4)
+SUM_ORDER = "xzxzxzxx"
+SPREAD_ORDER = "zxzxzzxzxzxz"
+SUM_LAGS = (0, 1, 5, 7, 9)
+SPREAD_LAGS = (0, 2, 4, 5)
+LATE_LAG = 8
 
 
 class Place:
@@ -43,7 +44,7 @@
 
     def greet(self):
         barrier = pltpu.get_barrier_semaphore()
-        peers = [self.partner(), self.opposite()] + [self.ring(k) for k in range(1, X_WAYS)]
+        peers = [self.partner(), self.opposite(), self.ring(1), self.ring(3)]
         for peer in peers:
             pl.semaphore_signal(barrier, inc=1, device_id=peer, device_id_type=MESH)
         pl.semaphore_wait(barrier, len(peers))
@@ -239,8 +240,6 @@
     )(packed, w_gate, w_up, w_down, weight)
 
 
-FAR_DP = ((2, 1), (1, 1), (3, 1), (2, 0), (0, 1), (1, 0), (3, 0))
-FAR_EXPERT = ((2, 1), (1, 1), (3, 1), (2, 0), (1, 0), (3, 0), (0, 1))
 Y_WAYS, PAIR = 4, 2
 
 
@@ -250,20 +249,44 @@
         self.d = (self.zh * X_WAYS + self.x) * CORES + self.c
         self.y, self.zl = self.expert % Y_WAYS, self.expert // Y_WAYS
 
-    def dp(self, far, core):
-        return ((self.zh + far[1]) % Z_WAYS * X_WAYS + (self.x + far[0]) % X_WAYS) * CORES + core
-
-    def other(self, far):
-        return (self.zl + far[1]) % PAIR * Y_WAYS + (self.y + far[0]) % Y_WAYS
-
-    def greet(self):
+    def along_y(self, k):
+        return (self.y + k) % Y_WAYS
+
+    def column(self, k):
+        return (self.zl * Y_WAYS + self.along_y(k), self.d)
+
+    def holder(self, pair, y_from, core):
+        return (pair * Y_WAYS + self.y, (self.zl * X_WAYS + y_from) * CORES + core)
+
+    def source(self, d):
+        return (self.zh * Y_WAYS + self.y, d)
+
+    def unless_self(self, peer, act):
+        @pl.when((peer[0] != self.expert) | (peer[1] != self.d))
+        def _():
+            act()
+
+    def greet(self, senders, others):
         barrier = pltpu.get_barrier_semaphore()
-        peers = [(self.other(far), self.d) for far in FAR_EXPERT]
-        peers += [(self.expert, self.dp(far, core)) for far in FAR_DP for core in range(CORES)]
-        peers.append(self.partner())
+        peers = [self.column(k) for k in range(1, Y_WAYS)] + others
         for peer in peers:
             pl.semaphore_signal(barrier, inc=1, device_id=peer, device_id_type=MESH)
-        pl.semaphore_wait(barrier, len(peers))
+        for peer in senders:
+            self.unless_self(
+                peer,
+                lambda peer=peer: pl.semaphore_signal(
+                    barrier, inc=1, device_id=peer, device_id_type=MESH
+                ),
+            )
+        pl.semaphore_wait(barrier, len(peers) + len(senders) - jnp.where(self.zl == self.zh, 1, 0))
+
+    def holders(self):
+        return [
+            self.holder(p, y, core) for p in range(PAIR) for y in range(Y_WAYS) for core in range(CORES)
+        ]
+
+    def sources(self):
+        return [self.source(d) for d in range(Z_WAYS * X_WAYS * CORES)]
 
 
 def dispatch_kernel(
@@ -274,69 +297,65 @@
     for h in range(CORES):
         cols = slice(h * shard, (h + 1) * shard)
         tok[h] = jnp.concatenate([x_ref[:, cols], g_ref[:, cols]], axis=1)
-    me.greet()
-
-    def picked(e, h):
-        return jnp.dot(pick_ref[e], tok[h], preferred_element_type=jnp.float32).astype(jnp.bfloat16)
-
-    def to_expert(h, k):
-        e = me.other(FAR_EXPERT[k])
+    me.greet(me.sources(), [])
+    pieces = [(q, h) for h in range(CORES) for q in range(PAIR)]
+
+    def pair(q):
+        return (1 - me.zh + q) % PAIR
+
+    def picked(q, h, y):
+        rows = jnp.dot(pick_ref[pair(q) * Y_WAYS + y], tok[h], preferred_element_type=jnp.float32)
+        return rows.astype(jnp.bfloat16)
+
+    def to_row(q, h, k):
         return remote(
-            away.at[h, e], mid.at[h, me.expert], send1.at[h, k], recv1.at[h, me.expert], (e, me.d)
+            away.at[h, me.along_y(k), pair(q)], mid.at[h, me.y, pair(q)],
+            send1.at[q, h, k - 1], recv1.at[q, h, me.y], me.column(k),
         )
 
-    def to_shard(h, k, d):
+    def to_holder(q, h, k):
+        y = me.along_y(k)
         return remote(
-            mid.at[h, d // CORES], out_ref.at[me.d // CORES, me.c], send2.at[h, k], recv2.at[me.d],
-            (me.expert, d),
+            mid.at[h, y, pair(q)], out_ref.at[me.d // CORES, me.c],
+            send2.at[q, h, k], recv2.at[me.d], me.holder(pair(q), y, h),
         )
 
-    for h in range(CORES):
-        for k, far in enumerate(FAR_EXPERT):
-            e = me.other(far)
-            away[h, e] = picked(e, h)
-            to_expert(h, k).start()
-        mid[h, me.expert] = picked(me.expert, h)
-
-    for h in range(CORES):
-        for k, far in enumerate(FAR_DP + ((0, 0),)):
-            d = me.dp(far, h)
-            src = d // CORES
-
-            @pl.when(src != me.expert)
+    for q, h in pieces:
+        for k in (2, 1, 3):
+            y = me.along_y(k)
+            away[h, y, pair(q)] = picked(q, h, y)
+            to_row(q, h, k).start()
+        mid[h, me.y, pair(q)] = picked(q, h, me.y)
+
+    for q, h in pieces:
+        for k in (0, 1, 3, 2):
+            y = me.along_y(k)
+            if k:
+                remote(
+                    away.at[h, y, pair(q)], mid.at[h, y, pair(q)],
+                    send1.at[q, h, 0], recv1.at[q, h, y], me.column(k),
+                ).wait_recv()
+            peer = me.holder(pair(q), y, h)
+            me.unless_self(peer, lambda q=q, h=h, k=k: to_holder(q, h, k).start())
+
+            @pl.when((peer[0] == me.expert) & (peer[1] == me.d))
             def _():
-                remote(
-                    away.at[h, src], mid.at[h, src], send1.at[h, 0], recv1.at[h, src], (src, me.d)
-                ).wait_recv()
-
-            if far != (0, 0):
-                to_shard(h, k, d).start()
-            else:
-
-                @pl.when(me.c != h)
-                def _():
-                    to_shard(h, k, d).start()
-
-                @pl.when(me.c == h)
-                def _():
-                    out_ref[me.d // CORES, me.c] = mid[h, src]
+                out_ref[me.d // CORES, me.c] = mid[h, y, pair(q)]
 
     def from_source(d):
-        return remote(mid.at[0, 0], out_ref.at[d // CORES, d % CORES], send2.at[0, 0], recv2.at[d], (me.expert, d))
-
-    for far in FAR_DP:
-        for core in range(CORES):
-            from_source(me.dp(far, core)).wait_recv()
-    from_source(me.dp((0, 0), 1 - me.c)).wait_recv()
-    for h in range(CORES):
-        for k, far in enumerate(FAR_EXPERT):
-            to_expert(h, k).wait_send()
-        for k, far in enumerate(FAR_DP):
-            to_shard(h, k, me.dp(far, h)).wait_send()
-
-        @pl.when(me.c != h)
-        def _():
-            to_shard(h, len(FAR_DP), me.dp((0, 0), h)).wait_send()
+        remote(
+            mid.at[0, 0, 0], out_ref.at[d // CORES, d % CORES], send2.at[0, 0, 0], recv2.at[d], me.source(d)
+        ).wait_recv()
+
+    for d in range(Z_WAYS * X_WAYS * CORES):
+        me.unless_self(me.source(d), lambda d=d: from_source(d))
+    for q, h in pieces:
+        for k in range(1, Y_WAYS):
+            to_row(q, h, k).wait_send()
+        for k in range(Y_WAYS):
+            me.unless_self(
+                me.holder(pair(q), me.along_y(k), h), lambda q=q, h=h, k=k: to_holder(q, h, k).wait_send()
+            )
 
 
 def spread_kernel(
@@ -344,7 +363,7 @@
     xt, gt, whole, total, dx, mid, back, send_sem, recv_sem, send1, recv1, send2, recv2,
 ):
     me = Wide()
-    me.greet()
+    me.greet(me.holders(), [me.partner(), me.opposite(), me.ring(1), me.ring(3)])
     n = wg_ref.shape[1] // CHUNKS
     blocks, rows, shard = X_WAYS * Z_WAYS, rows_ref.shape[2], wg_ref.shape[0]
     slots = CORES * blocks * rows
@@ -437,18 +456,15 @@
             to_partner(j).wait_recv()
             gd_ref[:, pl.ds((j - CHUNKS) * 2 * n, 2 * n)] = grad(gt, j, slice(0, 2 * n))
 
-    near = me.dp((0, 0), 1 - me.c)
-    targets = [me.dp(far, core) for far in FAR_DP for core in range(CORES)] + [near]
-
-    def to_block(k, d):
+    def to_source(d):
         return remote(
-            dx.at[d // CORES, d % CORES], mid.at[me.d // CORES, me.c], send1.at[k], recv1.at[me.d],
-            (me.expert, d),
+            dx.at[d // CORES, d % CORES], mid.at[me.x, me.zl, me.c], send1.at[d],
+            recv1.at[me.x, me.zl, me.c], me.source(d),
         )
 
-    def to_features(k):
-        e = me.other(FAR_EXPERT[k])
-        return remote(mid.at[e], back.at[me.expert], send2.at[k], recv2.at[me.expert], (e, me.d))
+    def to_column(k):
+        y = me.along_y(k)
+        return remote(mid.at[y], back.at[me.y], send2.at[k - 1], recv2.at[me.y], me.column(k))
 
     def home_first():
         for i in range(blocks):
@@ -457,40 +473,47 @@
                 one = total[at : at + rows // 2, :].astype(jnp.bfloat16)
                 two = total[at + rows // 2 : at + rows, :].astype(jnp.bfloat16)
                 dx[i, me.c if which == 0 else 1 - me.c] = jnp.concatenate([one, two], axis=1)
-        for k, d in enumerate(targets):
-            to_block(k, d).start()
-        mid[me.d // CORES, me.c] = dx[me.d // CORES, me.c]
-
-    def arrived(e):
-        for core in range(CORES):
-            d = e * CORES + core
-
-            @pl.when(d != me.d)
-            def _():
-                remote(
-                    dx.at[0, 0], mid.at[e, core], send1.at[0], recv1.at[d], (me.expert, d)
-                ).wait_recv()
+        for k in range(Z_WAYS * X_WAYS * CORES):
+            d = (me.d + k + 4) % (Z_WAYS * X_WAYS * CORES)
+            me.unless_self(me.source(d), lambda d=d: to_source(d).start())
+
+        @pl.when(me.zl == me.zh)
+        def _():
+            mid[me.x, me.zl, me.c] = dx[me.d // CORES, me.c]
+
+    def from_holder(p, y, core):
+        peer = me.holder(p, y, core)
+
+        def wait():
+            remote(
+                dx.at[0, 0], mid.at[y, p, core], send1.at[0], recv1.at[y, p, core], peer
+            ).wait_recv()
+
+        me.unless_self(peer, wait)
 
     def home_second():
-        for k, far in enumerate(FAR_EXPERT):
-            arrived(me.other(far))
-            to_features(k).start()
-        arrived(me.expert)
-        back[me.expert] = mid[me.expert]
+        for k in (2, 1, 3, 0):
+            y = me.along_y(k)
+            for p in range(PAIR):
+                for core in range(CORES):
+                    from_holder(p, y, core)
+            if k:
+                to_column(k).start()
+        back[me.y] = mid[me.y]
 
     def home():
-        for far in FAR_EXPERT:
-            e = me.other(far)
-            remote(mid.at[0], back.at[e], send2.at[0], recv2.at[e], (e, me.d)).wait_recv()
+        for k in range(1, Y_WAYS):
+            y = me.along_y(k)
+            remote(mid.at[0], back.at[y], send2.at[0], recv2.at[y], me.column(k)).wait_recv()
         parts = []
         for h in range(CORES):
-            blocks_of = back[:, h].reshape(low_ref.shape[1], CORES * shard)
+            blocks_of = back[:, :, h].reshape(low_ref.shape[1], CORES * shard)
             one = jnp.dot(low_ref[...], blocks_of, preferred_element_type=f32)
             two = jnp.dot(high_ref[...], blocks_of, preferred_element_type=f32)
             parts.append(one[:, :shard] + two[:, shard:])
         out_ref[...] = jnp.concatenate(parts, axis=1).astype(jnp.bfloat16)
 
-    for j in range(spread_chunks):
+    for j in range(CHUNKS):
         begin(j)
     for lo, turned in ((0, xt), (shard, gt)):
         for i in range(blocks):
@@ -501,33 +524,38 @@
         turned[...] = total[...].T.astype(jnp.bfloat16)
 
     def products(j):
-        if j < CHUNKS:
-            inputs(j)
+        inputs(j)
         if j == CHUNKS - 1:
             home_first()
-        if j < CHUNKS:
-            weights(j)
-
+        weights(j)
+
+    late = range(CHUNKS, spread_chunks)
     stages = (lambda j: middle(j, 0), lambda j: middle(j, 1), cores, products)
-    for t in range(spread_chunks + SPREAD_LAGS[-1]):
+    for t in range(CHUNKS + SPREAD_LAGS[-1]):
         for stage, lag in zip(stages, SPREAD_LAGS):
-            if 0 <= t - lag < spread_chunks:
+            if 0 <= t - lag < CHUNKS:
                 stage(t - lag)
+        if t - LATE_LAG in range(spread_chunks - CHUNKS):
+            begin(CHUNKS + t - LATE_LAG)
+    for stage in (stages[0], stages[1]):
+        for j in late:
+            stage(j)
     home_second()
-    for j in range(CHUNKS, spread_chunks):
-        weights(j)
+    for stage in (cores, weights):
+        for j in late:
+            stage(j)
     home()
     for j in range(spread_chunks):
         for one in [to_partner(j), opposite(j)] + neighbours(j) + passed(j):
             one.wait_send()
-    for k, d in enumerate(targets):
-        to_block(k, d).wait_send()
-    for k in range(len(FAR_EXPERT)):
-        to_features(k).wait_send()
+    for d in range(Z_WAYS * X_WAYS * CORES):
+        me.unless_self(me.source(d), lambda d=d: to_source(d).wait_send())
+    for k in range(1, Y_WAYS):
+        to_column(k).wait_send()
 
 
 def dispatched(pick, x, g):
-    (experts, rows, _), (tokens, width) = pick.shape, x.shape
+    (_, rows, _), (tokens, width) = pick.shape, x.shape
     bf16 = jnp.bfloat16
     groups = X_WAYS * Z_WAYS
     dma = pltpu.SemaphoreType.DMA
@@ -538,11 +566,11 @@
         out_specs=vmem(1)[0],
         scratch_shapes=[
             pltpu.VMEM((CORES, tokens, width), bf16),
-            pltpu.VMEM((CORES, experts, rows, width), bf16),
-            pltpu.VMEM((CORES, experts, rows, width), bf16),
-            dma((CORES, len(FAR_EXPERT))),
-            dma((CORES, experts)),
-            dma((CORES, len(FAR_DP) + 1)),
+            pltpu.VMEM((CORES, Y_WAYS, PAIR, rows, width), bf16),
+            pltpu.VMEM((CORES, Y_WAYS, PAIR, rows, width), bf16),
+            dma((PAIR, CORES, Y_WAYS - 1)),
+            dma((PAIR, CORES, Y_WAYS)),
+            dma((PAIR, CORES, Y_WAYS)),
             dma((groups * CORES,)),
         ],
         compiler_params=pltpu.CompilerParams(
@@ -555,7 +583,6 @@
     (blocks, cores, rows, width), (shard, hidden) = packed.shape, w_gate.shape
     cols = 2 * hidden // CHUNKS
     slots = cores * blocks * rows
-    experts = Y_WAYS * PAIR
     count = len(SPREAD_ORDER)
     bf16, dma = jnp.bfloat16, pltpu.SemaphoreType.DMA
     return pl.pallas_call(
@@ -574,14 +601,14 @@
             pltpu.VMEM((count, cores, Z_WAYS, X_WAYS, rows, cols), bf16),
             pltpu.VMEM((slots, shard), jnp.float32),
             pltpu.VMEM((blocks, cores, rows // 2, width), bf16),
-            pltpu.VMEM((experts, cores, rows // 2, width), bf16),
-            pltpu.VMEM((experts, cores, rows // 2, width), bf16),
+            pltpu.VMEM((Y_WAYS, PAIR, cores, rows // 2, width), bf16),
+            pltpu.VMEM((Y_WAYS, PAIR, cores, rows // 2, width), bf16),
             dma((count, 6)),
             dma((count, 6)),
             dma((blocks * cores,)),
-            dma((blocks * cores,)),
-            dma((len(FAR_EXPERT),)),
-            dma((experts,)),
+            dma((Y_WAYS, PAIR, cores)),
+            dma((Y_WAYS - 1,)),
+            dma((Y_WAYS,)),
         ],
         compiler_params=pltpu.CompilerParams(
             collective_id=1, has_side_effects=True, vmem_limit_bytes=50 << 20
@@ -610,7 +637,8 @@
     pick = chosen.astype(jnp.bfloat16)
 
     def place(first):
-        part = rank.T[:, :, None] == jnp.arange(first, first + capacity // 2, dtype=jnp.int32)
+        by_row = rank.reshape(PAIR, Y_WAYS, tok_rows).transpose(2, 1, 0).reshape(tok_rows, experts)
+        part = by_row[:, :, None] == jnp.arange(first, first + capacity // 2, dtype=jnp.int32)
         return part.astype(jnp.bfloat16).reshape(tok_rows, experts * capacity // 2)
 
     weight_of = jnp.where(hit0, route_weights[:, 0][None, :], 0.0) + jnp.where(

time: 213 us -> 198 us (0.930)
  the two profiles are of different devices: /device:TPU:1 before, /device:TPU:33 now
where the time goes in v5:
time: 198 us
  Pallas kernels  187 us (94%)
  local copies, waits for them, and re-layouts  10 us (5%)
    pallas_call x1, Pallas kernels, spread_rows(): pl.pallas_call(functools.partial(spread_kernel, inv_root), out_shape=(jax...  90.3 us
    pallas_call x1, Pallas kernels, summed_rows(): pl.pallas_call(sum_kernel, out_shape=jax.ShapeDtypeStruct((CHUNKS * 3 //...  60.8 us
    pallas_call x1, Pallas kernels, dispatched(): pl.pallas_call(dispatch_kernel, out_shape=jax.ShapeDtypeStruct((groups, C...  36 us
    unnamed x14, local copies, waits for them, and re-layouts  8.12 us

profile of v5, /device:TPU:33, one launch (start us, length us, event | category | flops | bytes accessed | tf_op | source)
XLA Modules:
  0.0 198.2 jit_solution(17697018929662524156)
XLA Ops:
  0.6 0.8 slice_bitcast_fusion.3
  1.4 0.8 slice_bitcast_fusion.1
  2.2 0.1 fusion
  2.3 0.1 select_reduce_fusion
  2.5 0.1 eq.119
  2.5 0.1 eq.115
  2.6 0.1 copy.16.pw_ref
  2.7 0.1 copy.18
  2.9 0.0 copy-start.1
  2.9 0.9 copy-done.1
  3.8 0.0 copy-start.2
  3.9 0.9 copy-done.2
  4.8 36.0 %shard_map.102.rows_ref = bf16[8,2,64,896]{3,2,1,0:T(8,128)(2,1)S(1)} custom-call(bf16[8,64,128]{2,1,0:T(8,128)(2,1)S(1)} %fusion.1.pick_ref, bf16[128,896]{1,0:T(8,128)(2,1)S(1)} %copy-done.1, bf16[128,896]{1,0:T(8,128)(2,1)S(1)} %copy-done.2), custom_call_target="tpu_custom_call" | custom-call | tf_op jit(solution)/shard_map/pallas_call | solution.py:562
  40.8 0.0 copy-start
  40.8 60.8 %shard_map.103.act_ref = bf16[12,64,512]{2,1,0:T(8,128)(2,1)S(1)} custom-call(bf16[8,2,64,896]{3,2,1,0:T(8,128)(2,1)S(1)} %shard_map.102.rows_ref, bf16[448,2048]{1,0:T(8,128)(2,1)} %bitcast.29, bf16[448,2048]{1,0:T(8,128)(2,1)} %bitcast.31, bf16[448,2048]{1,0:T(8,128)(2,1)} %bitcast.35, f32[64,1]{1,0:T(8,128)S(1)} %copy.16.pw_ref), custom_call_target="tpu_custom_call" | custom-call | tf_op jit(solution)/shard_map/pallas_call | solution.py:221
  101.6 0.0 copy-done
  101.7 90.3 %shard_map.104 = (bf16[448,2048]{1,0:T(8,128)(2,1)S(1)}, bf16[448,2048]{1,0:T(8,128)(2,1)}, bf16[448,2048]{1,0:T(8,128)(2,1)}, bf16[128,896]{1,0:T(8,128)(2,1)S(1)}) custom-call(bf16[12,64,512]{2,1,0:T(8,128)(2,1)S(1)} %shard_map.103.act_ref, bf16[8,2,64,896]{3,2,1,0:T(8,128)(2,1)} %copy-done, bf16[448,2048]{1,0:T(8,128)(2,1)} %bitcast.30, ...), custom_call_target="tpu_custom_call" | custom-call | tf_op jit(solution)/shard_map/pallas_call | solution.py:588
  192.0 0.7 copy.24
  192.7 0.0 copy-start.4
  192.7 1.2 copy.25
  193.9 0.9 copy-done.4
  194.8 1.2 copy.26
  196.0 0.9 copy-done.3
  197.0 1.2 copy.27
  (11 shorter events, 0.1 us)
Async XLA Ops:
  2.9 0.9 copy-start.1
  3.8 0.9 copy-start.2
  40.8 60.9 %copy-start = (bf16[8,2,64,896]{3,2,1,0:T(8,128)(2,1)}, bf16[8,2,64,896]{3,2,1,0:T(8,128)(2,1)S(1)}, u32[]{:S(2)}) copy-start(bf16[8,2,64,896]{3,2,1,0:T(8,128)(2,1)S(1)} %shard_map.102.rows_ref) | copy-start | bytes 5505028
  192.7 2.2 %copy-start.4 = (bf16[448,2048]{1,0:T(8,128)(2,1)S(1)}, bf16[448,2048]{1,0:T(8,128)(2,1)}, u32[]{:S(2)}) copy-start(bf16[448,2048]{1,0:T(8,128)(2,1)} %get-tuple-element.10) | copy-start | bytes 5505028
  194.8 2.2 %copy-start.3 = (bf16[448,2048]{1,0:T(8,128)(2,1)S(1)}, bf16[448,2048]{1,0:T(8,128)(2,1)}, u32[]{:S(2)}) copy-start(bf16[448,2048]{1,0:T(8,128)(2,1)} %get-tuple-element.11) | copy-start | bytes 5505028

commit v6 on v5

--- a/solution.py
+++ b/solution.py
@@ -12,8 +12,8 @@
 CHUNKS = 8
 X_WAYS, Z_WAYS, CORES = 4, 2, 2
 LAST = (((1,), (1,)), ((), ()))
-SUM_ORDER = "xzxzxzxx"
-SPREAD_ORDER = "zxzxzzxzxzxz"
+SUM_ORDER = "xzxzxxzx"
+SPREAD_ORDER = "xzxzzxzzzzzx"
 SUM_LAGS = (0, 1, 5, 7, 9)
 SPREAD_LAGS = (0, 2, 4, 5)
 LATE_LAG = 8
@@ -515,7 +515,7 @@
 
     for j in range(CHUNKS):
         begin(j)
-    for lo, turned in ((0, xt), (shard, gt)):
+    def turn(turned, lo):
         for i in range(blocks):
             for which in range(CORES):
                 at = pl.ds((which * blocks + i) * rows, rows)
@@ -523,27 +523,28 @@
                 total[at, :] = rows_ref[i, c][:, lo : lo + shard].astype(f32)
         turned[...] = total[...].T.astype(jnp.bfloat16)
 
-    def products(j):
-        inputs(j)
-        if j == CHUNKS - 1:
-            home_first()
-        weights(j)
-
     late = range(CHUNKS, spread_chunks)
-    stages = (lambda j: middle(j, 0), lambda j: middle(j, 1), cores, products)
+    stages = (lambda j: middle(j, 0), lambda j: middle(j, 1), cores, inputs)
     for t in range(CHUNKS + SPREAD_LAGS[-1]):
         for stage, lag in zip(stages, SPREAD_LAGS):
             if 0 <= t - lag < CHUNKS:
                 stage(t - lag)
         if t - LATE_LAG in range(spread_chunks - CHUNKS):
             begin(CHUNKS + t - LATE_LAG)
-    for stage in (stages[0], stages[1]):
-        for j in late:
-            stage(j)
+    home_first()
+    for j in late:
+        stages[0](j)
+    turn(xt, 0)
+    for j in late:
+        weights(2 * (j - CHUNKS))
+        stages[1](j)
+    turn(gt, shard)
     home_second()
-    for stage in (cores, weights):
-        for j in late:
-            stage(j)
+    for j in late:
+        cores(j)
+        weights(2 * (j - CHUNKS) + 1)
+    for j in late:
+        weights(j)
     home()
     for j in range(spread_chunks):
         for one in [to_partner(j), opposite(j)] + neighbours(j) + passed(j):

time: 198 us -> 192 us (0.970)
  the two profiles are of different devices: /device:TPU:33 before, /device:TPU:1 now
where the time goes in v6:
time: 192 us; the launch traced here: 189 us
  Pallas kernels  178 us (93%)
  local copies, waits for them, and re-layouts  10 us (5%)
    pallas_call x1, Pallas kernels, spread_rows(): pl.pallas_call(functools.partial(spread_kernel, inv_root), out_shape=(jax...  81.3 us
    pallas_call x1, Pallas kernels, summed_rows(): pl.pallas_call(sum_kernel, out_shape=jax.ShapeDtypeStruct((CHUNKS * 3 //...  59.6 us
    pallas_call x1, Pallas kernels, dispatched(): pl.pallas_call(dispatch_kernel, out_shape=jax.ShapeDtypeStruct((groups, C...  36.9 us
    unnamed x14, local copies, waits for them, and re-layouts  8.12 us

profile of v6, /device:TPU:1, one launch (start us, length us, event | category | flops | bytes accessed | tf_op | source)
XLA Modules:
  0.0 188.8 jit_solution(17032812429379664912)
XLA Ops:
  0.6 0.8 slice_bitcast_fusion.3
  1.4 0.8 slice_bitcast_fusion.1
  2.2 0.1 fusion
  2.3 0.1 select_reduce_fusion
  2.5 0.1 eq.119
  2.5 0.1 eq.115
  2.6 0.1 copy.16.pw_ref
  2.7 0.1 copy.18
  2.9 0.0 copy-start.1
  2.9 0.9 copy-done.1
  3.8 0.0 copy-start.2
  3.9 0.9 copy-done.2
  4.8 36.9 %shard_map.102.rows_ref = bf16[8,2,64,896]{3,2,1,0:T(8,128)(2,1)S(1)} custom-call(bf16[8,64,128]{2,1,0:T(8,128)(2,1)S(1)} %fusion.1.pick_ref, bf16[128,896]{1,0:T(8,128)(2,1)S(1)} %copy-done.1, bf16[128,896]{1,0:T(8,128)(2,1)S(1)} %copy-done.2), custom_call_target="tpu_custom_call" | custom-call | tf_op jit(solution)/shard_map/pallas_call | solution.py:563
  41.7 0.0 copy-start
  41.7 59.6 %shard_map.103.act_ref = bf16[12,64,512]{2,1,0:T(8,128)(2,1)S(1)} custom-call(bf16[8,2,64,896]{3,2,1,0:T(8,128)(2,1)S(1)} %shard_map.102.rows_ref, bf16[448,2048]{1,0:T(8,128)(2,1)} %bitcast.29, bf16[448,2048]{1,0:T(8,128)(2,1)} %bitcast.31, bf16[448,2048]{1,0:T(8,128)(2,1)} %bitcast.35, f32[64,1]{1,0:T(8,128)S(1)} %copy.16.pw_ref), custom_call_target="tpu_custom_call" | custom-call | tf_op jit(solution)/shard_map/pallas_call | solution.py:221
  101.3 0.0 copy-done
  101.3 81.3 %shard_map.104 = (bf16[448,2048]{1,0:T(8,128)(2,1)S(1)}, bf16[448,2048]{1,0:T(8,128)(2,1)}, bf16[448,2048]{1,0:T(8,128)(2,1)}, bf16[128,896]{1,0:T(8,128)(2,1)S(1)}) custom-call(bf16[12,64,512]{2,1,0:T(8,128)(2,1)S(1)} %shard_map.103.act_ref, bf16[8,2,64,896]{3,2,1,0:T(8,128)(2,1)} %copy-done, bf16[448,2048]{1,0:T(8,128)(2,1)} %bitcast.30, ...), custom_call_target="tpu_custom_call" | custom-call | tf_op jit(solution)/shard_map/pallas_call | solution.py:589
  182.6 0.7 copy.24
  183.3 0.0 copy-start.4
  183.3 1.2 copy.25
  184.5 0.9 copy-done.4
  185.4 1.2 copy.26
  186.7 0.9 copy-done.3
  187.6 1.2 copy.27
  (11 shorter events, 0.1 us)
Async XLA Ops:
  2.9 0.9 copy-start.1
  3.8 0.9 copy-start.2
  41.7 59.6 %copy-start = (bf16[8,2,64,896]{3,2,1,0:T(8,128)(2,1)}, bf16[8,2,64,896]{3,2,1,0:T(8,128)(2,1)S(1)}, u32[]{:S(2)}) copy-start(bf16[8,2,64,896]{3,2,1,0:T(8,128)(2,1)S(1)} %shard_map.102.rows_ref) | copy-start | bytes 5505028
  183.3 2.2 %copy-start.4 = (bf16[448,2048]{1,0:T(8,128)(2,1)S(1)}, bf16[448,2048]{1,0:T(8,128)(2,1)}, u32[]{:S(2)}) copy-start(bf16[448,2048]{1,0:T(8,128)(2,1)} %get-tuple-element.10) | copy-start | bytes 5505028
  185.4 2.2 %copy-start.3 = (bf16[448,2048]{1,0:T(8,128)(2,1)S(1)}, bf16[448,2048]{1,0:T(8,128)(2,1)}, u32[]{:S(2)}) copy-start(bf16[448,2048]{1,0:T(8,128)(2,1)} %get-tuple-element.11) | copy-start | bytes 5505028

commit v7 on v6

--- a/solution.py
+++ b/solution.py
@@ -14,8 +14,8 @@
 LAST = (((1,), (1,)), ((), ()))
 SUM_ORDER = "xzxzxxzx"
 SPREAD_ORDER = "xzxzzxzzzzzx"
-SUM_LAGS = (0, 1, 5, 7, 9)
-SPREAD_LAGS = (0, 2, 4, 5)
+SUM_LAGS = (0, 1, 4, 6, 8)
+SPREAD_LAGS = (2, 4, 6, 7)
 LATE_LAG = 8
 
 
@@ -57,12 +57,10 @@
     )
 
 
-def sum_kernel(
-    rows_ref, wg_ref, wu_ref, wd_ref, pw_ref, out_ref,
+def sum_stages(
+    me, rows_ref, wg_ref, wu_ref, wd_ref, pw_ref, out_ref,
     xp, gp, away, arrived, held, first, second, send_sem, recv_sem,
 ):
-    me = Place()
-    me.greet()
     n = wg_ref.shape[1] // CHUNKS
     blocks, rows, shard = X_WAYS * Z_WAYS, rows_ref.shape[2], wg_ref.shape[0]
     low, high = pl.ds(0, rows // 2), pl.ds(rows // 2, rows // 2)
@@ -99,8 +97,8 @@
 
     def opposite(j):
         if SUM_ORDER[j] == "x":
-            return copy(j, 1, held.at[j, 1 - me.zh, here], first.at[j, 4], me.opposite())
-        return copy(j, 1, held.at[j, 1 - me.zh], first.at[j, pl.ds(0, X_WAYS)], me.opposite())
+            return copy(j, 1, held.at[j, 1 - me.zh, here], second.at[j, 2], me.opposite())
+        return copy(j, 1, held.at[j, 1 - me.zh], first.at[j], me.opposite())
 
     def ring_first(j, lanes=(0, 1, 2, 3)):
         mine = held.at[j, me.zh]
@@ -184,7 +182,7 @@
         total = held[j, me.zh, here].astype(f32)
         if SUM_ORDER[j] == "x":
             arrive([opposite(j)])
-            total += first[j, 4].astype(f32)
+            total += second[j, 2].astype(f32)
         else:
             arrive(ring_first(j, (2, 3)) + ring_second(j))
             total += second[j, 0].astype(f32) + second[j, 1].astype(f32)
@@ -200,44 +198,15 @@
         order = (pass_on, gather) if SUM_ORDER[j] == "x" else (gather, pass_on)
         order[step](j)
 
-    stages = (make, cores, lambda j: middle(j, 0), lambda j: middle(j, 1), finish)
-    for t in range(CHUNKS + SUM_LAGS[-1]):
-        for stage, lag in zip(stages, SUM_LAGS):
-            if 0 <= t - lag < CHUNKS:
-                stage(t - lag)
-    for j in range(CHUNKS):
+    def sent(j):
         for one in [to_partner(j), opposite(j)] + ring_first(j) + ring_second(j):
             one.wait_send()
 
+    return (make, cores, lambda j: middle(j, 0), lambda j: middle(j, 1), finish), sent
+
 
 def vmem(count):
     return [pl.BlockSpec(memory_space=pltpu.VMEM)] * count
-
-
-def summed_rows(packed, w_gate, w_up, w_down, weight):
-    (blocks, cores, rows, _), (shard, hidden) = packed.shape, w_gate.shape
-    cols = 3 * hidden // CHUNKS
-    bf16 = jnp.bfloat16
-    return pl.pallas_call(
-        sum_kernel,
-        out_shape=jax.ShapeDtypeStruct((CHUNKS * 3 // 2, rows, 2 * hidden // CHUNKS), bf16),
-        in_specs=vmem(5),
-        out_specs=vmem(1)[0],
-        scratch_shapes=[
-            pltpu.VMEM((cores, blocks * rows, shard), bf16),
-            pltpu.VMEM((cores, blocks * rows, shard), bf16),
-            pltpu.VMEM((CHUNKS, Z_WAYS, X_WAYS, rows, cols), bf16),
-            pltpu.VMEM((CHUNKS, Z_WAYS, X_WAYS, rows, cols), bf16),
-            pltpu.VMEM((CHUNKS, Z_WAYS, X_WAYS, rows, cols), bf16),
-            pltpu.VMEM((CHUNKS, X_WAYS + 1, rows, cols), bf16),
-            pltpu.VMEM((CHUNKS, X_WAYS - 1, rows, cols), bf16),
-            pltpu.SemaphoreType.DMA((CHUNKS, 8)),
-            pltpu.SemaphoreType.DMA((CHUNKS, 8)),
-        ],
-        compiler_params=pltpu.CompilerParams(
-            collective_id=0, has_side_effects=True, vmem_limit_bytes=50 << 20
-        ),
-    )(packed, w_gate, w_up, w_down, weight)
 
 
 Y_WAYS, PAIR = 4, 2
@@ -358,12 +327,16 @@
             )
 
 
-def spread_kernel(
-    inv_root, act_ref, rows_ref, wg_ref, wu_ref, low_ref, high_ref, gg_ref, gu_ref, gd_ref, out_ref,
-    xt, gt, whole, total, dx, mid, back, send_sem, recv_sem, send1, recv1, send2, recv2,
+def expert_kernel(
+    inv_root, rows_ref, wg_ref, wu_ref, wd_ref, pw_ref, low_ref, high_ref, gg_ref, gu_ref, gd_ref, out_ref,
+    act_ref, xp, gp, away, arrived, held, first, second, sum_send, sum_recv, xt, gt, whole, total, dx, mid, back, send_sem, recv_sem, send1, recv1, send2, recv2,
 ):
     me = Wide()
     me.greet(me.holders(), [me.partner(), me.opposite(), me.ring(1), me.ring(3)])
+    sums, sums_sent = sum_stages(
+        me, rows_ref, wg_ref, wu_ref, wd_ref, pw_ref, act_ref,
+        xp, gp, away, arrived, held, first, second, sum_send, sum_recv,
+    )
     n = wg_ref.shape[1] // CHUNKS
     blocks, rows, shard = X_WAYS * Z_WAYS, rows_ref.shape[2], wg_ref.shape[0]
     slots = CORES * blocks * rows
@@ -513,8 +486,6 @@
             parts.append(one[:, :shard] + two[:, shard:])
         out_ref[...] = jnp.concatenate(parts, axis=1).astype(jnp.bfloat16)
 
-    for j in range(CHUNKS):
-        begin(j)
     def turn(turned, lo):
         for i in range(blocks):
             for which in range(CORES):
@@ -525,12 +496,14 @@
 
     late = range(CHUNKS, spread_chunks)
     stages = (lambda j: middle(j, 0), lambda j: middle(j, 1), cores, inputs)
-    for t in range(CHUNKS + SPREAD_LAGS[-1]):
-        for stage, lag in zip(stages, SPREAD_LAGS):
+    line = sums + (begin,) + stages
+    lags = SUM_LAGS + tuple(SUM_LAGS[-1] + lag for lag in (0,) + SPREAD_LAGS)
+    for t in range(CHUNKS + lags[-1]):
+        for stage, lag in zip(line, lags):
             if 0 <= t - lag < CHUNKS:
                 stage(t - lag)
-        if t - LATE_LAG in range(spread_chunks - CHUNKS):
-            begin(CHUNKS + t - LATE_LAG)
+        if t - SUM_LAGS[-1] - LATE_LAG in range(spread_chunks - CHUNKS):
+            begin(CHUNKS + t - SUM_LAGS[-1] - LATE_LAG)
     home_first()
     for j in late:
         stages[0](j)
@@ -546,6 +519,8 @@
     for j in late:
         weights(j)
     home()
+    for j in range(CHUNKS):
+        sums_sent(j)
     for j in range(spread_chunks):
         for one in [to_partner(j), opposite(j)] + neighbours(j) + passed(j):
             one.wait_send()
@@ -580,23 +555,33 @@
     )(pick, x, g)
 
 
-def spread_rows(inv_root, act, packed, w_gate, w_up, low, high):
+def expert_rows(inv_root, packed, w_gate, w_up, w_down, weight, low, high):
     (blocks, cores, rows, width), (shard, hidden) = packed.shape, w_gate.shape
-    cols = 2 * hidden // CHUNKS
+    cols, sum_cols = 2 * hidden // CHUNKS, 3 * hidden // CHUNKS
     slots = cores * blocks * rows
     count = len(SPREAD_ORDER)
     bf16, dma = jnp.bfloat16, pltpu.SemaphoreType.DMA
     return pl.pallas_call(
-        functools.partial(spread_kernel, inv_root),
+        functools.partial(expert_kernel, inv_root),
         out_shape=(
             jax.ShapeDtypeStruct((shard, hidden), bf16),
             jax.ShapeDtypeStruct((shard, hidden), bf16),
             jax.ShapeDtypeStruct((shard, hidden), bf16),
             jax.ShapeDtypeStruct((low.shape[0], width), bf16),
         ),
-        in_specs=vmem(6),
+        in_specs=vmem(7),
         out_specs=vmem(4),
         scratch_shapes=[
+            pltpu.VMEM((count, rows, cols), bf16),
+            pltpu.VMEM((cores, blocks * rows, shard), bf16),
+            pltpu.VMEM((cores, blocks * rows, shard), bf16),
+            pltpu.VMEM((CHUNKS, Z_WAYS, X_WAYS, rows, sum_cols), bf16),
+            pltpu.VMEM((CHUNKS, Z_WAYS, X_WAYS, rows, sum_cols), bf16),
+            pltpu.VMEM((CHUNKS, Z_WAYS, X_WAYS, rows, sum_cols), bf16),
+            pltpu.VMEM((CHUNKS, X_WAYS, rows, sum_cols), bf16),
+            pltpu.VMEM((CHUNKS, X_WAYS - 1, rows, sum_cols), bf16),
+            dma((CHUNKS, 8)),
+            dma((CHUNKS, 8)),
             pltpu.VMEM((shard, slots), bf16),
             pltpu.VMEM((shard, slots), bf16),
             pltpu.VMEM((count, cores, Z_WAYS, X_WAYS, rows, cols), bf16),
@@ -612,9 +597,9 @@
             dma((Y_WAYS,)),
         ],
         compiler_params=pltpu.CompilerParams(
-            collective_id=1, has_side_effects=True, vmem_limit_bytes=50 << 20
+            collective_id=0, has_side_effects=True, vmem_limit_bytes=59 << 20
         ),
-    )(act, packed, w_gate, w_up, low, high)
+    )(packed, w_gate, w_up, w_down, weight, low, high)
 
 
 def body(tokens, grad_out, expert_ids, route_weights, w_gate, w_up, w_down):
@@ -655,9 +640,9 @@
     )
 
     packed = dispatched(pick, tokens, grad_out)
-    act = summed_rows(packed, gate_shard, up_shard, down_shard, own_weight[:, None])
-    grad_g, grad_u, grad_d, grad_tokens = spread_rows(
-        inv_root, act, packed, gate_shard, up_shard, place(0), place(capacity // 2)
+    grad_g, grad_u, grad_d, grad_tokens = expert_rows(
+        inv_root, packed, gate_shard, up_shard, down_shard, own_weight[:, None],
+        place(0), place(capacity // 2),
     )
     return (grad_tokens, grad_g[None], grad_u[None], grad_d.T[None])
 

time: 192 us -> 187 us (0.974)
  the two profiles are of different devices: /device:TPU:1 before, /device:TPU:2 now
where the time goes in v7:
time: 187 us
  Pallas kernels  171 us (91%)
  local copies, waits for them, and re-layouts  13.7 us (7%)
    pallas_call x1, Pallas kernels, expert_rows(): pl.pallas_call(functools.partial(expert_kernel, inv_root), out_shape=(jax...  138 us
    pallas_call x1, Pallas kernels, dispatched(): pl.pallas_call(dispatch_kernel, out_shape=jax.ShapeDtypeStruct((groups, C...  33 us
    unnamed x14, local copies, waits for them, and re-layouts  11.2 us

profile of v7, /device:TPU:2, one launch (start us, length us, event | category | flops | bytes accessed | tf_op | source)
XLA Modules:
  0.0 186.6 jit_solution(4342505542370117074)
XLA Ops:
  0.6 0.8 slice_bitcast_fusion.3
  1.4 0.8 slice_bitcast_fusion.1
  2.2 0.1 fusion
  2.3 0.1 select_reduce_fusion
  2.5 0.1 eq.119
  2.5 0.1 eq.115
  2.6 0.7 copy.19.pw_ref
  3.3 0.1 copy.17
  3.4 0.7 compare_convert_fusion
  4.2 0.0 copy-start.1
  4.2 0.9 copy-done.1
  5.1 0.0 copy-start.2
  5.1 0.9 copy-done.2
  6.0 33.0 %shard_map.102.rows_ref = bf16[8,2,64,896]{3,2,1,0:T(8,128)(2,1)S(1)} custom-call(bf16[8,64,128]{2,1,0:T(8,128)(2,1)S(1)} %fusion.1.pick_ref, bf16[128,896]{1,0:T(8,128)(2,1)S(1)} %copy-done.1, bf16[128,896]{1,0:T(8,128)(2,1)S(1)} %copy-done.2), custom_call_target="tpu_custom_call" | custom-call | tf_op jit(solution)/shard_map/pallas_call | solution.py:538
  39.1 0.0 copy-start
  39.1 1.2 copy-done
  40.3 138.1 %shard_map.103 = (bf16[448,2048]{1,0:T(8,128)(2,1)}, bf16[448,2048]{1,0:T(8,128)(2,1)}, bf16[448,2048]{1,0:T(8,128)(2,1)}, bf16[128,896]{1,0:T(8,128)(2,1)}) custom-call(bf16[8,2,64,896]{3,2,1,0:T(8,128)(2,1)} %copy-done, bf16[448,2048]{1,0:T(8,128)(2,1)} %bitcast.28, bf16[448,2048]{1,0:T(8,128)(2,1)} %bitcast.29, bf16[448,2048]{1,0:T(8,128)(2,1)} %bitcast.30, ...), custom_call_target="tpu_custom_call" | custom-call | tf_op jit(solution)/shard_map/pallas_call | solution.py:564
  178.5 1.6 copy.24
  180.1 0.0 copy-start.4
  180.1 3.1 %copy.25 = bf16[1,448,2048]{2,1,0:T(8,128)(2,1)} copy(bf16[1,448,2048]{2,1,0:T(8,128)(2,1)} %bitcast.33) | data formatting | bytes 3670016
  183.2 0.0 copy-done.4
  183.2 1.2 copy.26
  184.4 0.9 copy-done.3
  185.4 1.2 copy.27
  (10 shorter events, 0.1 us)
Async XLA Ops:
  4.2 0.9 copy-start.1
  5.1 0.9 copy-start.2
  39.1 1.2 copy-start
  180.1 3.1 %copy-start.4 = (bf16[448,2048]{1,0:T(8,128)(2,1)S(1)}, bf16[448,2048]{1,0:T(8,128)(2,1)}, u32[]{:S(2)}) copy-start(bf16[448,2048]{1,0:T(8,128)(2,1)} %get-tuple-element.10) | copy-start | bytes 5505028
  183.2 2.2 %copy-start.3 = (bf16[448,2048]{1,0:T(8,128)(2,1)S(1)}, bf16[448,2048]{1,0:T(8,128)(2,1)}, u32[]{:S(2)}) copy-start(bf16[448,2048]{1,0:T(8,128)(2,1)} %get-tuple-element.11) | copy-start | bytes 5505028

commit v8 on v7

--- a/solution.py
+++ b/solution.py
@@ -511,8 +511,8 @@
     for j in late:
         weights(2 * (j - CHUNKS))
         stages[1](j)
+    home_second()
     turn(gt, shard)
-    home_second()
     for j in late:
         cores(j)
         weights(2 * (j - CHUNKS) + 1)

time: 187 us -> 186 us (level)
  the two profiles are of different devices: /device:TPU:2 before, /device:TPU:1 now
where the time goes in v8:
time: 186 us; the launch traced here: 182 us
  Pallas kernels  167 us (90%)
  local copies, waits for them, and re-layouts  13.7 us (7%)
    pallas_call x1, Pallas kernels, expert_rows(): pl.pallas_call(functools.partial(expert_kernel, inv_root), out_shape=(jax...  130 us
    pallas_call x1, Pallas kernels, dispatched(): pl.pallas_call(dispatch_kernel, out_shape=jax.ShapeDtypeStruct((groups, C...  36.9 us
    unnamed x14, local copies, waits for them, and re-layouts  11.2 us

profile of v8, /device:TPU:1, one launch (start us, length us, event | category | flops | bytes accessed | tf_op | source)
XLA Modules:
  0.0 182.5 jit_solution(7310685014902968667)
XLA Ops:
  0.6 0.8 slice_bitcast_fusion.3
  1.4 0.8 slice_bitcast_fusion.1
  2.2 0.1 fusion
  2.3 0.1 select_reduce_fusion
  2.5 0.1 eq.119
  2.5 0.1 eq.115
  2.6 0.7 copy.19.pw_ref
  3.3 0.1 copy.17
  3.4 0.7 compare_convert_fusion
  4.2 0.0 copy-start.1
  4.2 0.9 copy-done.1
  5.1 0.0 copy-start.2
  5.1 0.9 copy-done.2
  6.0 36.9 %shard_map.102.rows_ref = bf16[8,2,64,896]{3,2,1,0:T(8,128)(2,1)S(1)} custom-call(bf16[8,64,128]{2,1,0:T(8,128)(2,1)S(1)} %fusion.1.pick_ref, bf16[128,896]{1,0:T(8,128)(2,1)S(1)} %copy-done.1, bf16[128,896]{1,0:T(8,128)(2,1)S(1)} %copy-done.2), custom_call_target="tpu_custom_call" | custom-call | tf_op jit(solution)/shard_map/pallas_call | solution.py:538
  43.0 0.0 copy-start
  43.0 1.2 copy-done
  44.2 130.2 %shard_map.103 = (bf16[448,2048]{1,0:T(8,128)(2,1)}, bf16[448,2048]{1,0:T(8,128)(2,1)}, bf16[448,2048]{1,0:T(8,128)(2,1)}, bf16[128,896]{1,0:T(8,128)(2,1)}) custom-call(bf16[8,2,64,896]{3,2,1,0:T(8,128)(2,1)} %copy-done, bf16[448,2048]{1,0:T(8,128)(2,1)} %bitcast.28, bf16[448,2048]{1,0:T(8,128)(2,1)} %bitcast.29, bf16[448,2048]{1,0:T(8,128)(2,1)} %bitcast.30, ...), custom_call_target="tpu_custom_call" | custom-call | tf_op jit(solution)/shard_map/pallas_call | solution.py:564
  174.4 1.6 copy.24
  176.0 0.0 copy-start.4
  176.0 3.1 %copy.25 = bf16[1,448,2048]{2,1,0:T(8,128)(2,1)} copy(bf16[1,448,2048]{2,1,0:T(8,128)(2,1)} %bitcast.33) | data formatting | bytes 3670016
  179.1 0.0 copy-done.4
  179.1 1.2 copy.26
  180.3 0.9 copy-done.3
  181.2 1.2 copy.27
  (10 shorter events, 0.1 us)
Async XLA Ops:
  4.2 0.9 copy-start.1
  5.1 0.9 copy-start.2
  43.0 1.2 copy-start
  176.0 3.1 %copy-start.4 = (bf16[448,2048]{1,0:T(8,128)(2,1)S(1)}, bf16[448,2048]{1,0:T(8,128)(2,1)}, u32[]{:S(2)}) copy-start(bf16[448,2048]{1,0:T(8,128)(2,1)} %get-tuple-element.10) | copy-start | bytes 5505028
  179.1 2.2 %copy-start.3 = (bf16[448,2048]{1,0:T(8,128)(2,1)S(1)}, bf16[448,2048]{1,0:T(8,128)(2,1)}, u32[]{:S(2)}) copy-start(bf16[448,2048]{1,0:T(8,128)(2,1)} %get-tuple-element.11) | copy-start | bytes 5505028
